TPU v7x, 256 devices: a whole 4x4x8 slice. The times are simulated.
256 devices in a mesh: row: 64 (over y, z, core), col: 4 (over x).
Axes of the slice: x: 4, y: 4, z: 8, core: 2. Of those that a mesh axis runs over, the one named last changes fastest.
Arguments:
- grad_out: bfloat16 [524288, 512], P('row', 'col'), may hold values from -6 to 6
- features: bfloat16 [524288, 512], P('row', 'col')
- weight: bfloat16 [512, 512], P(None, 'col'), may hold values from -0.25 to 0.25
- tiles: bfloat16 [12288, 128, 128], P('row'), may hold values from -0.75 to 0.75
- tile_row_block: int32 [12288], P('row'), may hold values from 0 to 63
- tile_owner: int32 [12288, 1], P('row'), may hold values from 0 to 63; in each aligned block of 192 rows (0 to 191, 192 to 383, ...) at most 4 rows name the same one
- tile_local: int32 [12288], P('row'), may hold values from 0 to 63
- degrees: int32 [524288], P('row'), may hold values from 1 to 8
- live: int32 [64], P('row'), may hold values from 1 to 192, 9216 in all
Outputs:
- grad_pre: bfloat16 [524288, 512], P('row', 'col')
- grad_weight: float32 [512, 512], P(None, 'col')
Inputs may be any that keep to these rules, and one draw needn't show every extreme that they name: `tile_owner`: within the 192 tile slots of one index of row, no owner is named more than 4 times, and 4 is reached in some index of row. Some index of row has all 192 slots live.
All inputs are finite; a program needn't handle non-finite values. No bound on the sum of `live` on one device may be relied on, other than what follows from the above.
Results may differ from a plain program's by a relative error of at most 0.0061.
Values may be sent and summed in bfloat16 or wider, within the bound.
No kernel may reach another device: no remote copies, remote signals or barrier semaphores. Data moves between devices by JAX's collectives and lax.ppermute only.
A program may use at most 128 MiB of HBM per device.

v0:
```python
import math

import jax
import jax.numpy as jnp
from jax import lax
from jax.sharding import PartitionSpec as P


def per_device(
    grad_out, features, weight, tiles, tile_row_block, tile_owner, tile_local, degrees, live
):
    node_rows, width_cols = grad_out.shape
    tile_size = tiles.shape[1]
    tile_count = tiles.shape[0]
    blocks = node_rows // tile_size
    peers = lax.axis_size("row")
    capacity = max(2, 4 * tile_count // (3 * peers))
    scale = lax.rsqrt(degrees.astype(jnp.float32))
    scaled = (grad_out.astype(jnp.float32) * scale[:, None]).astype(jnp.bfloat16)
    source_features = scaled.reshape(blocks, tile_size, width_cols)[tile_row_block]
    tile_product = jnp.einsum(
        "tkr,tkc->trc", tiles, source_features, preferred_element_type=jnp.float32
    ).astype(jnp.bfloat16)
    alive = jnp.arange(tile_count) < live[0]
    owner = tile_owner[:, 0]
    member = (owner[:, None] == jnp.arange(peers)[None, :]).astype(jnp.int32)
    before = jnp.cumsum(member, axis=0) - member
    place = jnp.sum(before * member, axis=1)
    slot_index = jnp.where(alive, owner * capacity + place, peers * capacity)
    outgoing = (
        jnp.zeros((peers * capacity, tile_size, width_cols), jnp.bfloat16)
        .at[slot_index]
        .set(tile_product, mode="drop")
    )
    labels = (
        jnp.full((peers * capacity,), -1, jnp.int32).at[slot_index].set(tile_local, mode="drop")
    )
    outgoing = outgoing.reshape(peers, capacity, tile_size, width_cols)
    labels = labels.reshape(peers, capacity)
    incoming, in_labels = (
        lax.all_to_all(outgoing, "row", split_axis=0, concat_axis=0, tiled=True),
        lax.all_to_all(labels, "row", split_axis=0, concat_axis=0, tiled=True),
    )
    incoming = incoming.reshape(peers * capacity, tile_size * width_cols)
    selector = (in_labels.reshape(-1)[None, :] == jnp.arange(blocks)[:, None]).astype(jnp.bfloat16)
    summed_partials = jnp.dot(selector, incoming, preferred_element_type=jnp.float32).reshape(
        node_rows, width_cols
    )
    propagated = (summed_partials * scale[:, None]).astype(jnp.bfloat16)
    norm_factor = 1.0 / math.sqrt(node_rows * peers)
    local_terms = lax.dot_general(
        lax.all_gather(features, "col", axis=1, tiled=True),
        propagated,
        (((0,), (0,)), ((), ())),
        preferred_element_type=jnp.float32,
    )
    grad_weight = lax.psum(local_terms, "row") * norm_factor
    partial_back = lax.dot_general(
        propagated, weight, (((1,), (1,)), ((), ())), preferred_element_type=jnp.float32
    )
    back = lax.psum_scatter(partial_back, "col", scatter_dimension=1, tiled=True)
    grad_pre = jnp.where(features > 0, back, 0.0).astype(jnp.bfloat16)
    return (grad_pre, grad_weight)


def solution(mesh):
    return jax.shard_map(
        per_device,
        mesh=mesh,
        in_specs=(
            P("row", "col"),
            P("row", "col"),
            P(None, "col"),
            P("row", None, None),
            P("row"),
            P("row", None),
            P("row"),
            P("row"),
            P("row"),
        ),
        out_specs=(P("row", "col"), P(None, "col")),
        check_vma=False,
    )
```

profile of v0, /device:TPU:1, one launch (start us, length us, event | category | flops | bytes accessed | tf_op | source)
XLA Modules:
  0.0 642.7 jit_solution(6546624739221379363)
XLA Ops:
  7.2 0.7 iota_compare_fusion.1
  8.9 0.7 fusion.4
  10.9 1.3 scatter_custom_fusion
  12.3 0.7 all_to_all.9
  13.0 13.2 %all-to-all-start = ((s32[64,1,4]{2,1,0:T(1,128)}), s32[64,1,4]{2,1,0:T(1,128)S(1)}, u32[]{:S(2)}, u32[]{:S(2)}) async-start(s32[64,1,4]{2,1,0:T(1,128)} %bitcast.5), calls=%async_computation | async-start | bytes 65536 | tf_op jit(solution)/shard_map/all_to_all | solution.py:42
  26.2 0.8 convert_rsqrt_fusion
  27.6 2.5 multiply_convert_fusion.1
  30.1 8.1 %gather_fusion = bf16[192,128,128]{2,1,0:T(8,128)(2,1)} fusion(bf16[64,128,128]{2,1,0:T(8,128)(2,1)S(1)} %bitcast.34, s32[1024]{0:T(1024)S(1)} %pad_clamp_fusion), kind=kCustom, calls=%fused_computation | custom fusion | bytes 12583680 | tf_op jit(solution)/shard_map/gather | solution.py:20
  38.2 9.5 %convert_bitcast_fusion = bf16[192,128,128]{1,2,0:T(8,128)(2,1)} fusion(bf16[192,128,128]{2,1,0:T(8,128)(2,1)} %gather_fusion, bf16[192,128,128]{2,1,0:T(8,128)(2,1)} %param.12), kind=kOutput, calls=%fused_computation.6 | convolution fusion | flops 808452096 | bytes 18874368 | tf_op jit(solution)/shard_map/tkr,tkc->trc/dot_general | solution.py:21
  47.6 8.7 %copy.22 = bf16[192,128,128]{2,1,0:T(8,128)(2,1)} copy(bf16[192,128,128]{1,2,0:T(8,128)(2,1)} %convert_bitcast_fusion) | data formatting | bytes 12582912 | tf_op jit(solution)/shard_map/convert_element_type | solution.py:23
  56.3 5.3 broadcast_in_dim.25
  61.6 28.7 %scatter_fusion = bf16[256,128,128]{2,1,0:T(8,128)(2,1)} fusion(bf16[256,128,128]{2,1,0:T(8,128)(2,1)} %broadcast_in_dim.25, s32[192]{0:T(256)S(1)} %bitcast.38, bf16[192,128,128]{2,1,0:T(8,128)(2,1)} %copy.22), kind=kCustom, calls=%fused_computation.2 | custom fusion | bytes 18875136 | tf_op jit(solution)/shard_map/scatter | solution.py:33
  90.3 10.3 %all-to-all-start.1 = ((bf16[64,4,128,128]{3,2,1,0:T(8,128)(2,1)}), bf16[64,4,128,128]{3,2,1,0:T(8,128)(2,1)}, u32[]{:S(2)}, u32[]{:S(2)}) async-start(bf16[64,4,128,128]{3,2,1,0:T(8,128)(2,1)} %bitcast.33), calls=%async_computation.1 | async-start | bytes 16777216 | tf_op jit(solution)/shard_map/all_to_all | solution.py:41
  102.1 0.7 reduce.5
  103.0 183.5 %all-to-all-done.1 = bf16[64,4,128,128]{3,2,1,0:T(8,128)(2,1)} async-done(((bf16[64,4,128,128]{3,2,1,0:T(8,128)(2,1)}), bf16[64,4,128,128]{3,2,1,0:T(8,128)(2,1)}, u32[]{:S(2)}, u32[]{:S(2)}) %all-to-all-start.1) | async-done | bytes 8388640 | tf_op jit(solution)/shard_map/all_to_all | solution.py:41
  286.4 10.3 %fusion = f32[64,16384]{1,0:T(8,128)} fusion(bf16[32,8,128,128]{3,2,1,0:T(8,128)(2,1)} %bitcast.15, s32[256]{0:T(256)S(1)} %eq.44), kind=kOutput, calls=%fused_computation.3 | convolution fusion | flops 536887296 | bytes 12583936 | tf_op jit(solution)/shard_map/dot_general | solution.py:46
  296.8 4.9 reshape.47
  301.6 7.9 %convolution_bitcast_fusion = f32[512,128]{0,1:T(8,128)} fusion(bf16[8192,512]{1,0:T(8,128)(2,1)} %all-gather.2.cloned.1.call-done, f32[8192,128]{1,0:T(8,128)} %reshape.47, f32[8192]{0:T(1024)S(1)} %convert_rsqrt_fusion), kind=kOutput, calls=%fused_computation.10 | convolution fusion | flops 1075838976 | bytes 12877824 | tf_op jit(solution)/shard_map/dot_general | solution.py:51
  309.7 8.7 %fusion.8 = f32[8192,512]{1,0:T(8,128)} fusion(bf16[512,128]{1,0:T(8,128)(2,1)S(1)} %copy-done, f32[8192,128]{1,0:T(8,128)} %reshape.47, f32[8192]{0:T(1024)S(1)} %convert_rsqrt_fusion), kind=kOutput, calls=%fused_computation.31 | convolution fusion | flops 1075838976 | bytes 21135360 | tf_op jit(solution)/shard_map/dot_general | solution.py:58
  318.3 163.3 %all-reduce.3.cloned.1.call-done = f32[512,128]{0,1:T(8,128)} async-done(((f32[512,128]{0,1:T(8,128)}), f32[512,128]{0,1:T(8,128)}) %all-reduce.3.cloned.1.call-update) | async-done | bytes 262160 | tf_op jit(solution)/shard_map/psum | solution.py:57
  481.6 1.0 broadcast_multiply_fusion
  482.6 0.8 copy.23
  483.5 148.7 %reduce-scatter.2.cloned.1.call-done = f32[8192,128]{1,0:T(8,128)} async-done(((f32[8192,512]{1,0:T(8,128)}), f32[8192,128]{1,0:T(8,128)}) %reduce-scatter.2.cloned.1.call-update) | async-done | bytes 4194320 | tf_op jit(solution)/shard_map/reduce_scatter | solution.py:61
  632.1 4.0 select_convert_fusion
  (23 shorter events, 4.0 us)
Async XLA Ops:
  7.2 302.5 %copy-start = (bf16[512,128]{1,0:T(8,128)(2,1)S(1)}, bf16[512,128]{1,0:T(8,128)(2,1)}, u32[]{:S(2)}) copy-start(bf16[512,128]{1,0:T(8,128)(2,1)} %param.11) | copy-start | bytes 393220
  13.0 77.3 %all-to-all-start = ((s32[64,1,4]{2,1,0:T(1,128)}), s32[64,1,4]{2,1,0:T(1,128)S(1)}, u32[]{:S(2)}, u32[]{:S(2)}) async-start(s32[64,1,4]{2,1,0:T(1,128)} %bitcast.5), calls=%async_computation | async-start | bytes 65536 | tf_op jit(solution)/shard_map/all_to_all | solution.py:42
  90.3 196.1 %all-to-all-start.1 = ((bf16[64,4,128,128]{3,2,1,0:T(8,128)(2,1)}), bf16[64,4,128,128]{3,2,1,0:T(8,128)(2,1)}, u32[]{:S(2)}, u32[]{:S(2)}) async-start(bf16[64,4,128,128]{3,2,1,0:T(8,128)(2,1)} %bitcast.33), calls=%async_computation.1 | async-start | bytes 16777216 | tf_op jit(solution)/shard_map/all_to_all | solution.py:41
  100.7 201.0 %all-gather.2.cloned.1.call-start = ((), (), s32[]{:S(2)}) async-start(), calls=%async_computation.4 | async-start | bytes 10485760 | tf_op jit(solution)/shard_map/all_gather | solution.py:52
  101.4 380.2 %all-reduce.3.cloned.1.call-start = ((), (), s32[]{:S(2)}) async-start(), calls=%async_computation.5 | async-start | bytes 524288 | tf_op jit(solution)/shard_map/psum | solution.py:57
  309.6 322.5 %reduce-scatter.2.cloned.1.call-start = ((), (), s32[]{:S(2)}) async-start(), calls=%async_computation.3 | async-start | bytes 20971520 | tf_op jit(solution)/shard_map/reduce_scatter | solution.py:61
  318.3 313.8 %copy-start.1 = (bf16[8192,128]{1,0:T(8,128)(2,1)S(1)}, bf16[8192,128]{1,0:T(8,128)(2,1)}, u32[]{:S(2)}) copy-start(bf16[8192,128]{1,0:T(8,128)(2,1)} %param.10) | copy-start | bytes 6291460
Sparse Core Ops, SparseCore 0:
  103.3 89.7 all-gather.1
  309.7 171.8 all-reduce.2
  484.4 147.6 reduce-scatter.1
where the time goes:
time: 644 us; the launch traced here: 643 us
  waiting for transfers between devices  496 us (77%)
  local copies, waits for them, and re-layouts  59.3 us (9%)
  matrix products  36.4 us (6%)
  starting transfers between devices  23.8 us (4%)
  between operations  14.5 us (2%)
  other arithmetic  12.6 us (2%)
    all_to_all x1, waiting for transfers between devices, per_device(): lax.all_to_all(outgoing, 'row', split_axis=0, concat_axis=0, tiled=True)  183 us
    psum x1, waiting for transfers between devices, per_device(): grad_weight = lax.psum(local_terms, 'row') * norm_factor  163 us
    reduce_scatter x1, waiting for transfers between devices, per_device(): lax.psum_scatter(partial_back, 'col', scatter_dimension=1, tiled=True)  149 us
    scatter x1, local copies, waits for them, and re-layouts, per_device(): outgoing = jnp.zeros((peers * capacity, tile_size, width_cols), jnp.bfloa...  28.7 us
    all_to_all x1, starting transfers between devices, per_device(): lax.all_to_all(labels, 'row', split_axis=0, concat_axis=0, tiled=True)  13.2 us
  transfers between devices with their start and end apart: 5, of which 3 were waited for; matrix products, arithmetic and copies ran while one was open for 14% of the time, Pallas kernels for 0%

commit v1 on v0

v1 whole, which is shorter than its diff:
```python
import functools
import math

import jax
import jax.numpy as jnp
from jax import lax
from jax.experimental import pallas as pl
from jax.experimental.pallas import tpu as pltpu
from jax.sharding import PartitionSpec as P

PLACES = 4
LABEL_ROWS = 16
SPLIT = (64, 64)
VMEM = 48 * 1024 * 1024


def product_kernel(
    row_block, owner, local, live, tiles, scaled, out, count, labels, *, first, rows, group, label
):
    step = pl.program_id(0)
    size = tiles.shape[1]

    @pl.when(step == 0)
    def _():
        def clear(i, carry):
            count[i] = 0
            return carry

        lax.fori_loop(0, out.shape[0], clear, 0)
        if label:
            labels[...] = jnp.full(labels.shape, -1.0, labels.dtype)

    lane = lax.broadcasted_iota(jnp.int32, (LABEL_ROWS, size), 1)
    for i in range(group):
        tile = step * group + i
        peer = owner[tile]
        place = count[peer]
        count[peer] = place + 1
        source = scaled[pl.ds(pl.multiple_of(row_block[tile] * size, size), size), :]
        product = lax.dot_general(
            tiles[i, :, first : first + rows],
            source,
            (((0,), (0,)), ((), ())),
            preferred_element_type=jnp.float32,
        )
        out[peer, pl.ds(pl.multiple_of(place * rows, rows), rows), :] = product.astype(out.dtype)
        if label:
            value = jnp.where(tile < live[0], local[tile], -1).astype(jnp.float32)
            old = labels[peer].astype(jnp.float32)
            labels[peer] = jnp.where(lane == place, value, old).astype(labels.dtype)

    if label:

        @pl.when(step == pl.num_programs(0) - 1)
        def _():
            out[:, PLACES * rows :, :] = labels[...]


def products(row_block, owner, local, live, tiles, scaled, peers, first, rows, label):
    tile_count, size, _ = tiles.shape
    width = scaled.shape[1]
    group = 16
    extra = LABEL_ROWS if label else 0
    return pl.pallas_call(
        functools.partial(product_kernel, first=first, rows=rows, group=group, label=label),
        grid_spec=pltpu.PrefetchScalarGridSpec(
            num_scalar_prefetch=4,
            grid=(tile_count // group,),
            in_specs=[
                pl.BlockSpec((group, size, size), lambda i, *_: (i, 0, 0)),
                pl.BlockSpec(scaled.shape, lambda i, *_: (0, 0)),
            ],
            out_specs=pl.BlockSpec((peers, PLACES * rows + extra, width), lambda i, *_: (0, 0, 0)),
            scratch_shapes=[
                pltpu.SMEM((peers,), jnp.int32),
                pltpu.VMEM((peers, LABEL_ROWS, width), jnp.bfloat16),
            ],
        ),
        out_shape=jax.ShapeDtypeStruct((peers, PLACES * rows + extra, width), jnp.bfloat16),
        compiler_params=pltpu.CompilerParams(vmem_limit_bytes=VMEM),
        cost_estimate=pl.CostEstimate(
            flops=2 * tile_count * size * rows * width,
            bytes_accessed=2 * tiles.size + 2 * scaled.size + 2 * peers * PLACES * rows * width,
            transcendentals=0,
        ),
        name="products",
    )(row_block, owner, local, live, tiles, scaled)


def sum_kernel(labels, incoming, scale, low, high, total, *, rows, group):
    step = pl.program_id(0)
    half = low.shape[0]

    @pl.when(step == 0)
    def _():
        total[...] = jnp.zeros_like(total)

    for i in range(group):
        for place in range(PLACES):
            block = labels[(step * group + i) * PLACES + place]
            total[block] += incoming[i, place * rows : (place + 1) * rows, :].astype(jnp.float32)

    @pl.when(step == pl.num_programs(0) - 1)
    def _():
        low[...] = (total[:half] * scale[:half]).astype(low.dtype)
        high[...] = (total[half : 2 * half] * scale[half:]).astype(high.dtype)


def sums(labels, incoming, scale, rows):
    peers, depth, width = incoming.shape
    blocks = scale.shape[0]
    group = 8
    return pl.pallas_call(
        functools.partial(sum_kernel, rows=rows, group=group),
        grid_spec=pltpu.PrefetchScalarGridSpec(
            num_scalar_prefetch=1,
            grid=(peers // group,),
            in_specs=[
                pl.BlockSpec((group, depth, width), lambda i, *_: (i, 0, 0)),
                pl.BlockSpec(scale.shape, lambda i, *_: (0, 0, 0)),
            ],
            out_specs=[pl.BlockSpec((blocks // 2, rows, width), lambda i, *_: (0, 0, 0))] * 2,
            scratch_shapes=[pltpu.VMEM((blocks + 1, rows, width), jnp.float32)],
        ),
        out_shape=[jax.ShapeDtypeStruct((blocks // 2, rows, width), jnp.bfloat16)] * 2,
        compiler_params=pltpu.CompilerParams(vmem_limit_bytes=VMEM),
        cost_estimate=pl.CostEstimate(
            flops=incoming.size,
            bytes_accessed=2 * incoming.size + 4 * scale.size + 2 * scale.size,
            transcendentals=0,
        ),
        name="sums",
    )(labels, incoming, scale)


def back_kernel(*refs, half):
    low, high, (weight, features), out = refs[:4], refs[4:8], refs[8:10], refs[-1]
    rows, width = features.shape[1:]
    nodes = features.shape[0] * rows

    def run(parts):
        whole = jnp.concatenate([part[...].reshape(nodes, width) for part in parts], axis=1)
        back = lax.dot_general(
            whole, weight[...], (((1,), (0,)), ((), ())), preferred_element_type=jnp.float32
        ).reshape(features.shape)
        mask = features[...].astype(jnp.float32) > 0
        out[...] = jnp.where(mask, back, 0.0).astype(out.dtype)

    @pl.when(pl.program_id(0) < half)
    def _():
        run(low)

    @pl.when(pl.program_id(0) >= half)
    def _():
        run(high)


def back(low, high, weight, features, before, first, rows):
    blocks, size, width = features.shape
    steps = 4
    group = blocks // steps
    half = steps // 2
    spot = first // rows
    piece = pl.BlockSpec((group, rows, width), lambda i: (i, spot, 0))
    specs = [pl.BlockSpec((group, rows, width), lambda i: (jnp.minimum(i, half - 1), 0, 0))] * 4
    specs += [pl.BlockSpec((group, rows, width), lambda i: (jnp.maximum(i - half, 0), 0, 0))] * 4
    specs += [pl.BlockSpec(weight.shape, lambda i: (0, 0)), piece]
    args = [*low, *high, weight, features]
    aliases = {}
    if before is not None:
        specs.append(pl.BlockSpec(memory_space=pl.ANY))
        args.append(before)
        aliases = {len(args) - 1: 0}
    return pl.pallas_call(
        functools.partial(back_kernel, half=half),
        grid=(steps,),
        in_specs=specs,
        out_specs=piece,
        out_shape=jax.ShapeDtypeStruct(features.shape, jnp.bfloat16),
        input_output_aliases=aliases,
        compiler_params=pltpu.CompilerParams(vmem_limit_bytes=VMEM),
        cost_estimate=pl.CostEstimate(
            flops=2 * blocks * rows * width * weight.shape[0],
            bytes_accessed=2 * blocks * rows * (weight.shape[0] + 2 * width),
            transcendentals=0,
        ),
        name="back",
    )(*args)


def ring(shift, size):
    return [(i, (i + shift) % size) for i in range(size)]


def exchange(block):
    return lax.all_to_all(block, "row", split_axis=0, concat_axis=0, tiled=True)


def col_gather(low, high):
    size = lax.axis_size("col")
    ahead, behind = ring(1, size), ring(-1, size)
    low_left = lax.ppermute(low, "col", ahead)
    high_right = lax.ppermute(high, "col", behind)
    high_left = lax.ppermute(high, "col", ahead)
    low_right = lax.ppermute(low, "col", behind)
    low_far = lax.ppermute(low_left, "col", ahead)
    high_far = lax.ppermute(high_right, "col", behind)
    return (low, low_left, low_far, low_right), (high, high_left, high_far, high_right)


def weight_rows(weight):
    size = lax.axis_size("col")
    width = weight.shape[1]
    me = lax.axis_index("col")
    parts = []
    for shift in range(size):
        start = lax.rem(me + shift, size) * width
        slab = lax.dynamic_slice_in_dim(weight, start, width, 0)
        parts.append(slab if shift == 0 else lax.ppermute(slab, "col", ring(shift, size)))
    return jnp.concatenate(parts, axis=1).T


def per_device(
    grad_out, features, weight, tiles, tile_row_block, tile_owner, tile_local, degrees, live
):
    node_rows, width = grad_out.shape
    size = tiles.shape[1]
    blocks = node_rows // size
    peers = lax.axis_size("row")
    cols = lax.axis_size("col")
    scale = lax.rsqrt(degrees.astype(jnp.float32))
    scaled = (grad_out.astype(jnp.float32) * scale[:, None]).astype(jnp.bfloat16)
    owner = tile_owner[:, 0]
    weight_mine = weight_rows(weight)
    blocked = features.reshape(blocks, size, width)
    wide_scale = jnp.broadcast_to(scale.reshape(blocks, size, 1), (blocks, size, width))

    starts = [sum(SPLIT[:k]) for k in range(len(SPLIT))]
    gathered = lax.all_gather(features, "col", axis=0).reshape(cols, blocks, size, width)
    outgoing = [
        products(tile_row_block, owner, tile_local, live, tiles, scaled, peers, first, rows, k == 0)
        for k, (first, rows) in enumerate(zip(starts, SPLIT))
    ]
    outgoing[1], weight_mine, gathered = lax.optimization_barrier(
        (outgoing[1], weight_mine, gathered)
    )
    incoming = [exchange(each) for each in outgoing]

    tags = incoming[0][:, PLACES * SPLIT[0], :PLACES].astype(jnp.int32).reshape(-1)
    tags = jnp.where(tags < 0, blocks, tags)
    scales = [wide_scale[:, first : first + rows] for first, rows in zip(starts, SPLIT)]
    grad_pre = None
    terms = jnp.zeros((cols, width, width), jnp.float32)
    for k, (first, rows) in enumerate(zip(starts, SPLIT)):
        if k > 0:
            incoming[k], grad_pre, terms, scales[k] = lax.optimization_barrier(
                (incoming[k], grad_pre, terms, scales[k])
            )
        low, high = sums(tags, incoming[k], scales[k], rows)
        low, high = col_gather(low, high)
        propagated = jnp.concatenate([low[0], high[0]], axis=0)
        terms = terms + lax.dot_general(
            gathered[:, :, first : first + rows],
            propagated,
            (((1, 2), (0, 1)), ((), ())),
            preferred_element_type=jnp.float32,
        )
        grad_pre = back(low, high, weight_mine, blocked, grad_pre, first, rows)

    norm_factor = 1.0 / math.sqrt(node_rows * peers)
    share = cols * width // peers
    total = jnp.sum(exchange(terms.reshape(peers, share, width)), axis=0) * norm_factor
    total = jnp.broadcast_to(total.astype(jnp.bfloat16)[None], (peers, share, width))
    grad_weight = exchange(total).astype(jnp.float32)
    return (grad_pre.reshape(node_rows, width), grad_weight.reshape(cols * width, width))


def solution(mesh):
    return jax.shard_map(
        per_device,
        mesh=mesh,
        in_specs=(
            P("row", "col"),
            P("row", "col"),
            P(None, "col"),
            P("row", None, None),
            P("row"),
            P("row", None),
            P("row"),
            P("row"),
            P("row"),
        ),
        out_specs=(P("row", "col"), P(None, "col")),
        check_vma=False,
    )
```

time: 644 us -> 305 us (0.47)
  waiting for transfers between devices: 496 us -> 170 us
  local copies, waits for them, and re-layouts: 59.3 us -> 1.88 us
  Pallas kernels: 0 us -> 45.8 us
  matrix products: 36.4 us -> 4.78 us
  starting transfers between devices: 23.8 us -> 43.5 us
  blocking collectives: 0 us -> 16.8 us
  other arithmetic: 12.6 us -> 5.81 us
    psum x1 -> x0, waiting for transfers between devices: 163 us -> none  [per_device(): grad_weight = lax.psum(local_terms, 'row') * norm_factor]
    reduce_scatter x1 -> x0, waiting for transfers between devices: 149 us -> none  [per_device(): lax.psum_scatter(partial_back, 'col', scatter_dimension=1, tiled=True)]
    all_to_all x2 -> x3, waiting for transfers between devices: 183 us -> 93.2 us  [exchange(): return lax.all_to_all(block, 'row', split_axis=0, concat_axis=0, tiled=True)]
    all_gather x1, waiting for transfers between devices: 0.01 us -> 46.2 us  [per_device(): lax.all_gather(features, 'col', axis=0).reshape(cols, blocks, size, width)]
    pallas_call x0 -> x6, Pallas kernels: none -> 45.8 us  [the longest x2 24.8 us: products(): pl.pallas_call(functools.partial(product_kernel, first=first, rows=rows,...]
    dot_general x4 -> x2, matrix products: 36.4 us -> 4.78 us  [per_device(): lax.dot_general(gathered[:, :, first:first + rows], propagated, (((1, 2),...]
    scatter x2 -> x0, local copies, waits for them, and re-layouts: 30 us -> none  [the longest x1 28.7 us: per_device(): outgoing = jnp.zeros((peers * capacity, tile_size, width_cols), jnp.bfloa...]
    ppermute x0 -> x15, waiting for transfers between devices: none -> 29.9 us  [the longest x2 11.2 us: col_gather(): low_far = lax.ppermute(low_left, 'col', ahead)]
  transfers between devices with their start and end apart: 5 -> 19, of which waited for: 3 -> 8; matrix products, arithmetic and copies ran while one was open for 14% -> 4% of each run, Pallas kernels for 0% -> 12%
where the time goes in v1:
time: 305 us; the launch traced here: 303 us
  waiting for transfers between devices  170 us (56%)
  Pallas kernels  45.8 us (15%)
  starting transfers between devices  43.5 us (14%)
  blocking collectives  16.8 us (6%)
  between operations  14.9 us (5%)
  other arithmetic  5.81 us (2%)
  matrix products  4.78 us (2%)
    all_to_all x3, waiting for transfers between devices, exchange(): return lax.all_to_all(block, 'row', split_axis=0, concat_axis=0, tiled=True)  93.2 us
    all_gather x1, waiting for transfers between devices, per_device(): lax.all_gather(features, 'col', axis=0).reshape(cols, blocks, size, width)  46.2 us
    all_to_all x3, starting transfers between devices, exchange(): return lax.all_to_all(block, 'row', split_axis=0, concat_axis=0, tiled=True)  25.7 us
    pallas_call x2, Pallas kernels, products(): pl.pallas_call(functools.partial(product_kernel, first=first, rows=rows,...  24.8 us
    all_to_all x1, blocking collectives, exchange(): return lax.all_to_all(block, 'row', split_axis=0, concat_axis=0, tiled=True)  16.8 us
    pallas_call x2, Pallas kernels, sums(): pl.pallas_call(functools.partial(sum_kernel, rows=rows, group=group), gri...  12.5 us
    ppermute x2, waiting for transfers between devices, col_gather(): low_far = lax.ppermute(low_left, 'col', ahead)  11.2 us
    ppermute x2, waiting for transfers between devices, col_gather(): low_left = lax.ppermute(low, 'col', ahead)  10.1 us
  transfers between devices with their start and end apart: 19, of which 8 were waited for; matrix products, arithmetic and copies ran while one was open for 4% of the time, Pallas kernels for 12%

profile of v1, /device:TPU:1, one launch (start us, length us, event | category | flops | bytes accessed | tf_op | source)
XLA Modules:
  0.0 303.4 jit_solution(10838141218600502739)
XLA Ops:
  9.3 2.5 multiply_convert_fusion.scaled
  11.9 11.4 %products.2 = bf16[64,272,128]{2,1,0:T(8,128)(2,1)} custom-call(s32[192]{0:T(256)S(1)} %copy-done, s32[192]{0:T(256)S(1)} %bitcast.24, s32[192]{0:T(256)S(1)} %copy-done.2, s32[1]{0:T(128)S(6)} %copy.27.live, bf16[192,128,128]{2,1,0:T(8,128)(2,1)} %tiles.3, bf16[8192,128]{1,0:T(8,128)(2,1)S(1)} %multiply_convert_fusion.scaled), custom_call_target="tpu_custom_call" | custom-call | flops 402653184 | bytes 12582912 | tf_op jit(solution)/shard_map/products/pallas_call | solution.py:64
  23.3 13.5 %all-to-all-start = ((bf16[64,272,128]{2,1,0:T(8,128)(2,1)}), bf16[64,272,128]{2,1,0:T(8,128)(2,1)}, u32[]{:S(2)}, u32[]{:S(2)}) async-start(bf16[64,272,128]{2,1,0:T(8,128)(2,1)} %products.2), calls=%async_computation | async-start | bytes 8912896 | tf_op jit(solution)/shard_map/all_to_all | solution.py:196
  37.0 2.6 collective-permute-start.2
  41.2 13.4 %products.3 = bf16[64,256,128]{2,1,0:T(8,128)(2,1)} custom-call(s32[192]{0:T(256)S(1)} %copy-done, s32[192]{0:T(256)S(1)} %bitcast.25, s32[192]{0:T(256)S(1)} %copy-done.2, s32[1]{0:T(128)S(6)} %copy.27.live, bf16[192,128,128]{2,1,0:T(8,128)(2,1)} %tiles.3, bf16[8192,128]{1,0:T(8,128)(2,1)S(1)} %multiply_convert_fusion.scaled), custom_call_target="tpu_custom_call" | custom-call | flops 402653184 | bytes 12582912 | tf_op jit(solution)/shard_map/products/pallas_call | solution.py:64
  54.6 46.2 %all-gather.3.cloned.1.call-done = bf16[32768,128]{1,0:T(8,128)(2,1)} async-done(((bf16[8192,128]{1,0:T(8,128)(2,1)}), bf16[32768,128]{1,0:T(8,128)(2,1)}) %all-gather.3.cloned.1.call-update) | async-done | bytes 8388624 | tf_op jit(solution)/shard_map/all_gather | solution.py:239
  100.7 37.6 %all-to-all-done.incoming = bf16[64,272,128]{2,1,0:T(8,128)(2,1)} async-done(((bf16[64,272,128]{2,1,0:T(8,128)(2,1)}), bf16[64,272,128]{2,1,0:T(8,128)(2,1)}, u32[]{:S(2)}, u32[]{:S(2)}) %all-to-all-start) | async-done | bytes 4456480 | tf_op jit(solution)/shard_map/all_to_all | solution.py:196
  138.3 6.1 %all-to-all-start.1 = ((bf16[64,256,128]{2,1,0:T(8,128)(2,1)}), bf16[64,256,128]{2,1,0:T(8,128)(2,1)}, u32[]{:S(2)}, u32[]{:S(2)}) async-start(bf16[64,256,128]{2,1,0:T(8,128)(2,1)} %products.3), calls=%async_computation.1 | async-start | bytes 8388608 | tf_op jit(solution)/shard_map/all_to_all | solution.py:196
  146.2 6.6 %sums.2 = (bf16[32,64,128]{2,1,0:T(8,128)(2,1)S(1)}, bf16[32,64,128]{2,1,0:T(8,128)(2,1)S(1)}) custom-call(s32[256]{0:T(256)S(1)} %compare_select_fusion.labels, bf16[64,272,128]{2,1,0:T(8,128)(2,1)} %all-to-all-done.incoming, f32[64,64,128]{2,1,0:T(8,128)S(1)} %broadcast_in_dim.22.scale), custom_call_target="tpu_custom_call" | custom-call | flops 2228224 | bytes 7602176 | tf_op jit(solution)/shard_map/sums/pallas_call | solution.py:113
  154.1 1.4 collective-permute-start.7
  157.0 10.1 %collective-permute-done.3.refs_1_ = bf16[32,64,128]{2,1,0:T(8,128)(2,1)S(1)} collective-permute-done((bf16[32,64,128]{2,1,0:T(8,128)(2,1)S(1)}, bf16[32,64,128]{2,1,0:T(8,128)(2,1)S(1)}, u32[]{:S(2)}, u32[]{:S(2)}) %collective-permute-start.3) | collective-permute-done | bytes 524320 | tf_op jit(solution)/shard_map/ppermute | solution.py:202
  167.2 2.7 collective-permute-start.8
  169.8 8.3 %collective-permute-done.5.refs_3_ = bf16[32,64,128]{2,1,0:T(8,128)(2,1)S(1)} collective-permute-done((bf16[32,64,128]{2,1,0:T(8,128)(2,1)S(1)}, bf16[32,64,128]{2,1,0:T(8,128)(2,1)S(1)}, u32[]{:S(2)}, u32[]{:S(2)}) %collective-permute-start.5) | collective-permute-done | bytes 524320 | tf_op jit(solution)/shard_map/ppermute | solution.py:205
  178.4 11.2 %collective-permute-done.4.refs_2_ = bf16[32,64,128]{2,1,0:T(8,128)(2,1)S(1)} collective-permute-done((bf16[32,64,128]{2,1,0:T(8,128)(2,1)S(1)}, bf16[32,64,128]{2,1,0:T(8,128)(2,1)S(1)}, u32[]{:S(2)}, u32[]{:S(2)}) %collective-permute-start.4) | collective-permute-done | bytes 524320 | tf_op jit(solution)/shard_map/ppermute | solution.py:206
  189.6 4.2 %back.2.refs_10_ = bf16[64,128,128]{2,1,0:T(8,128)(2,1)} custom-call(bf16[32,64,128]{2,1,0:T(8,128)(2,1)S(1)} %get-tuple-element.14.refs_0_, bf16[32,64,128]{2,1,0:T(8,128)(2,1)S(1)} %collective-permute-done.3.refs_1_, bf16[32,64,128]{2,1,0:T(8,128)(2,1)S(1)} %collective-permute-done.4.refs_2_, bf16[32,64,128]{2,1,0:T(8,128)(2,1)S(1)} %collective-permute-done.5.refs_3_, ...), custom_call_target="tpu_custom_call" | custom-call | flops 536870912 | bytes 6291456 | tf_op jit(solution)/shard_map/back/pallas_call | solution.py:174
  195.1 45.2 %all-to-all-done.1.incoming = bf16[64,256,128]{2,1,0:T(8,128)(2,1)} async-done(((bf16[64,256,128]{2,1,0:T(8,128)(2,1)}), bf16[64,256,128]{2,1,0:T(8,128)(2,1)}, u32[]{:S(2)}, u32[]{:S(2)}) %all-to-all-start.1) | async-done | bytes 4194336 | tf_op jit(solution)/shard_map/all_to_all | solution.py:196
  240.9 6.0 %sums.3 = (bf16[32,64,128]{2,1,0:T(8,128)(2,1)S(1)}, bf16[32,64,128]{2,1,0:T(8,128)(2,1)S(1)}) custom-call(s32[256]{0:T(256)S(1)} %compare_select_fusion.labels, bf16[64,256,128]{2,1,0:T(8,128)(2,1)} %all-to-all-done.1.incoming, f32[64,64,128]{2,1,0:T(8,128)S(1)} %broadcast_in_dim.23.scale), custom_call_target="tpu_custom_call" | custom-call | flops 2097152 | bytes 7340032 | tf_op jit(solution)/shard_map/sums/pallas_call | solution.py:113
  248.1 1.4 collective-permute-start.13
  249.6 3.5 %fusion.7 = f32[4,128,128]{2,1,0:T(8,128)S(1)} fusion(bf16[4,64,128,128]{3,2,1,0:T(8,128)(2,1)} %bitcast.29, bf16[32,64,128]{2,1,0:T(8,128)(2,1)S(1)} %get-tuple-element.21.refs_4_, bf16[32,64,128]{2,1,0:T(8,128)(2,1)S(1)} %get-tuple-element.20.refs_0_), kind=kOutput, calls=%fused_computation.6 | convolution fusion | flops 537395200 | bytes 5505024 | tf_op jit(solution)/shard_map/dot_general | solution.py:262
  253.8 6.2 %all-to-all-start.2 = ((f32[64,8,128]{2,1,0:T(8,128)}), f32[64,8,128]{2,1,0:T(8,128)S(1)}, u32[]{:S(2)}, u32[]{:S(2)}) async-start(f32[64,8,128]{2,1,0:T(8,128)} %bitcast.12), calls=%async_computation.2 | async-start | bytes 524288 | tf_op jit(solution)/shard_map/all_to_all | solution.py:196
  261.5 10.5 %all-to-all-done.2 = f32[64,8,128]{2,1,0:T(8,128)S(1)} async-done(((f32[64,8,128]{2,1,0:T(8,128)}), f32[64,8,128]{2,1,0:T(8,128)S(1)}, u32[]{:S(2)}, u32[]{:S(2)}) %all-to-all-start.2) | async-done | bytes 262176 | tf_op jit(solution)/shard_map/all_to_all | solution.py:196
  272.2 2.7 collective-permute-start.14
  274.9 16.8 %all_to_all.20 = bf16[64,8,128]{2,1,0:T(8,128)(2,1)S(1)} all-to-all(bf16[64,8,128]{2,1,0:T(8,128)(2,1)S(1)} %broadcast_in_dim.24), channel_id=1, replica_groups=mesh['row'=64,'col'=4] {'row'}, dimensions={0} | all-to-all | bytes 262144 | tf_op jit(solution)/shard_map/all_to_all | solution.py:196
  292.4 4.2 %back.3 = bf16[64,128,128]{2,1,0:T(8,128)(2,1)} custom-call(bf16[32,64,128]{2,1,0:T(8,128)(2,1)S(1)} %get-tuple-element.20.refs_0_, bf16[32,64,128]{2,1,0:T(8,128)(2,1)S(1)} %collective-permute-done.9.refs_1_, bf16[32,64,128]{2,1,0:T(8,128)(2,1)S(1)} %collective-permute-done.10.refs_2_, ...), custom_call_target="tpu_custom_call", output_to_operand_aliasing={{}: (10, {})} | custom-call | flops 536870912 | bytes 6291456 | tf_op jit(solution)/shard_map/back/pallas_call | solution.py:174
  (56 shorter events, 14.6 us)
Async XLA Ops:
  7.2 4.7 %copy-start = (s32[192]{0:T(256)S(1)}, s32[192]{0:T(256)}, u32[]{:S(2)}) copy-start(s32[192]{0:T(256)} %row_block.3) | copy-start | bytes 2308
  7.2 4.7 %copy-start.1 = (s32[192,1]{0,1:T(1,128)S(1)}, s32[192,1]{0,1:T(1,128)}, u32[]{:S(2)}) copy-start(s32[192,1]{0,1:T(1,128)} %param.14) | copy-start | bytes 2308
  7.2 93.5 %all-gather.3.cloned.1.call-start = ((), (), s32[]{:S(2)}) async-start(), calls=%async_computation.4 | async-start | bytes 10485760 | tf_op jit(solution)/shard_map/all_gather | solution.py:239
  23.3 13.5 %copy-start.3 = (bf16[512,128]{1,0:T(8,128)(2,1)S(1)}, bf16[512,128]{1,0:T(8,128)(2,1)}, u32[]{:S(2)}) copy-start(bf16[512,128]{1,0:T(8,128)(2,1)} %param.11) | copy-start | bytes 393220
  23.3 115.0 %all-to-all-start = ((bf16[64,272,128]{2,1,0:T(8,128)(2,1)}), bf16[64,272,128]{2,1,0:T(8,128)(2,1)}, u32[]{:S(2)}, u32[]{:S(2)}) async-start(bf16[64,272,128]{2,1,0:T(8,128)(2,1)} %products.2), calls=%async_computation | async-start | bytes 8912896 | tf_op jit(solution)/shard_map/all_to_all | solution.py:196
  37.0 17.6 %collective-permute-start.2 = (bf16[128,128]{0,1:T(8,128)(2,1)S(1)}, bf16[128,128]{0,1:T(8,128)(2,1)S(1)}, u32[]{:S(2)}, u32[]{:S(2)}) collective-permute-start(bf16[128,128]{0,1:T(8,128)(2,1)S(1)} %copy.25), channel_id=1, source_target_pairs={{0,3},{1,0},{2,1},{3,2},{4,7},{5,4},{6,5},{7,6},{8,11},{9,8},{10,9... | collective-permute-start | bytes 98312 | tf_op jit(solution)/shard_map/ppermute | solution.py:219
  39.6 14.9 %collective-permute-start.1 = (bf16[128,128]{0,1:T(8,128)(2,1)S(1)}, bf16[128,128]{0,1:T(8,128)(2,1)S(1)}, u32[]{:S(2)}, u32[]{:S(2)}) collective-permute-start(bf16[128,128]{0,1:T(8,128)(2,1)S(1)} %copy.24), channel_id=1, source_target_pairs={{0,2},{1,3},{2,0},{3,1},{4,6},{5,7},{6,4},{7,5},{8,10},{9,11},{10,... | collective-permute-start | bytes 98312 | tf_op jit(solution)/shard_map/ppermute | solution.py:219
  40.4 14.2 %collective-permute-start = (bf16[128,128]{0,1:T(8,128)(2,1)S(1)}, bf16[128,128]{0,1:T(8,128)(2,1)S(1)}, u32[]{:S(2)}, u32[]{:S(2)}) collective-permute-start(bf16[128,128]{0,1:T(8,128)(2,1)S(1)} %copy.23), channel_id=1, source_target_pairs={{0,1},{1,2},{2,3},{3,0},{4,5},{5,6},{6,7},{7,4},{8,9},{9,10},{10,1... | collective-permute-start | bytes 98312 | tf_op jit(solution)/shard_map/ppermute | solution.py:219
  138.3 102.0 %all-to-all-start.1 = ((bf16[64,256,128]{2,1,0:T(8,128)(2,1)}), bf16[64,256,128]{2,1,0:T(8,128)(2,1)}, u32[]{:S(2)}, u32[]{:S(2)}) async-start(bf16[64,256,128]{2,1,0:T(8,128)(2,1)} %products.3), calls=%async_computation.1 | async-start | bytes 8388608 | tf_op jit(solution)/shard_map/all_to_all | solution.py:196
  145.6 48.2 %slice-start = ((s8[8388608]{0:T(1024)(128)(4,1)}), s8[4194304]{0:T(1024)(128)(4,1)S(1)}, s32[]{:S(2)}) async-start(s8[8388608]{0:T(1024)(128)(4,1)} %bitcast.30), calls=%async_computation.5 | async-start | bytes 8388608
  146.2 47.6 %slice-start.1 = ((s8[8388608]{0:T(1024)(128)(4,1)}), s8[4194304]{0:T(1024)(128)(4,1)S(1)}, s32[]{:S(2)}) async-start(s8[8388608]{0:T(1024)(128)(4,1)} %bitcast.30), calls=%async_computation.6 | async-start | bytes 8388608
  152.8 14.3 %collective-permute-start.3 = (bf16[32,64,128]{2,1,0:T(8,128)(2,1)S(1)}, bf16[32,64,128]{2,1,0:T(8,128)(2,1)S(1)}, u32[]{:S(2)}, u32[]{:S(2)}) collective-permute-start(bf16[32,64,128]{2,1,0:T(8,128)(2,1)S(1)} %get-tuple-element.14.refs_0_), channel_id=1, source_target_pairs={{0,1},{1,2},{2,3},{3,0},{4,5},{5,6},{6,7},{7,4},{8,9},{9,10},{10,1... | collective-permute-start | bytes 1572872 | tf_op jit(solution)/shard_map/ppermute | solution.py:202
  154.1 13.1 %collective-permute-start.7 = (bf16[32,64,128]{2,1,0:T(8,128)(2,1)S(1)}, bf16[32,64,128]{2,1,0:T(8,128)(2,1)S(1)}, u32[]{:S(2)}, u32[]{:S(2)}) collective-permute-start(bf16[32,64,128]{2,1,0:T(8,128)(2,1)S(1)} %get-tuple-element.15.refs_4_), channel_id=1, source_target_pairs={{0,3},{1,0},{2,1},{3,2},{4,7},{5,4},{6,5},{7,6},{8,11},{9,8},{10,9... | collective-permute-start | bytes 1572872 | tf_op jit(solution)/shard_map/ppermute | solution.py:203
  155.5 22.5 %collective-permute-start.5 = (bf16[32,64,128]{2,1,0:T(8,128)(2,1)S(1)}, bf16[32,64,128]{2,1,0:T(8,128)(2,1)S(1)}, u32[]{:S(2)}, u32[]{:S(2)}) collective-permute-start(bf16[32,64,128]{2,1,0:T(8,128)(2,1)S(1)} %get-tuple-element.14.refs_0_), channel_id=1, source_target_pairs={{0,3},{1,0},{2,1},{3,2},{4,7},{5,4},{6,5},{7,6},{8,11},{9,8},{10,9... | collective-permute-start | bytes 1572872 | tf_op jit(solution)/shard_map/ppermute | solution.py:205
  156.8 21.5 %collective-permute-start.6 = (bf16[32,64,128]{2,1,0:T(8,128)(2,1)S(1)}, bf16[32,64,128]{2,1,0:T(8,128)(2,1)S(1)}, u32[]{:S(2)}, u32[]{:S(2)}) collective-permute-start(bf16[32,64,128]{2,1,0:T(8,128)(2,1)S(1)} %get-tuple-element.15.refs_4_), channel_id=1, source_target_pairs={{0,1},{1,2},{2,3},{3,0},{4,5},{5,6},{6,7},{7,4},{8,9},{9,10},{10,1... | collective-permute-start | bytes 1572872 | tf_op jit(solution)/shard_map/ppermute | solution.py:204
  167.1 22.5 %collective-permute-start.4 = (bf16[32,64,128]{2,1,0:T(8,128)(2,1)S(1)}, bf16[32,64,128]{2,1,0:T(8,128)(2,1)S(1)}, u32[]{:S(2)}, u32[]{:S(2)}) collective-permute-start(bf16[32,64,128]{2,1,0:T(8,128)(2,1)S(1)} %collective-permute-done.3.refs_1_), channel_id=1, source_target_pairs={{0,1},{1,2},{2,3},{3,0},{4,5},{5,6},{6,7},{7,4},{8,9},{9,10},{10,1... | collective-permute-start | bytes 1572872 | tf_op jit(solution)/shard_map/ppermute | solution.py:206
  167.2 22.5 %collective-permute-start.8 = (bf16[32,64,128]{2,1,0:T(8,128)(2,1)S(1)}, bf16[32,64,128]{2,1,0:T(8,128)(2,1)S(1)}, u32[]{:S(2)}, u32[]{:S(2)}) collective-permute-start(bf16[32,64,128]{2,1,0:T(8,128)(2,1)S(1)} %collective-permute-done.7.refs_7_), channel_id=1, source_target_pairs={{0,3},{1,0},{2,1},{3,2},{4,7},{5,4},{6,5},{7,6},{8,11},{9,8},{10,9... | collective-permute-start | bytes 1572872 | tf_op jit(solution)/shard_map/ppermute | solution.py:207
  246.8 25.2 %collective-permute-start.9 = (bf16[32,64,128]{2,1,0:T(8,128)(2,1)S(1)}, bf16[32,64,128]{2,1,0:T(8,128)(2,1)S(1)}, u32[]{:S(2)}, u32[]{:S(2)}) collective-permute-start(bf16[32,64,128]{2,1,0:T(8,128)(2,1)S(1)} %get-tuple-element.20.refs_0_), channel_id=1, source_target_pairs={{0,1},{1,2},{2,3},{3,0},{4,5},{5,6},{6,7},{7,4},{8,9},{9,10},{10,1... | collective-permute-start | bytes 1572872 | tf_op jit(solution)/shard_map/ppermute | solution.py:202
  248.1 24.0 %collective-permute-start.13 = (bf16[32,64,128]{2,1,0:T(8,128)(2,1)S(1)}, bf16[32,64,128]{2,1,0:T(8,128)(2,1)S(1)}, u32[]{:S(2)}, u32[]{:S(2)}) collective-permute-start(bf16[32,64,128]{2,1,0:T(8,128)(2,1)S(1)} %get-tuple-element.21.refs_4_), channel_id=1, source_target_pairs={{0,3},{1,0},{2,1},{3,2},{4,7},{5,4},{6,5},{7,6},{8,11},{9,8},{10,9... | collective-permute-start | bytes 1572872 | tf_op jit(solution)/shard_map/ppermute | solution.py:203
  253.8 18.2 %all-to-all-start.2 = ((f32[64,8,128]{2,1,0:T(8,128)}), f32[64,8,128]{2,1,0:T(8,128)S(1)}, u32[]{:S(2)}, u32[]{:S(2)}) async-start(f32[64,8,128]{2,1,0:T(8,128)} %bitcast.12), calls=%async_computation.2 | async-start | bytes 524288 | tf_op jit(solution)/shard_map/all_to_all | solution.py:196
  260.0 32.3 %collective-permute-start.11 = (bf16[32,64,128]{2,1,0:T(8,128)(2,1)S(1)}, bf16[32,64,128]{2,1,0:T(8,128)(2,1)S(1)}, u32[]{:S(2)}, u32[]{:S(2)}) collective-permute-start(bf16[32,64,128]{2,1,0:T(8,128)(2,1)S(1)} %get-tuple-element.20.refs_0_), channel_id=1, source_target_pairs={{0,3},{1,0},{2,1},{3,2},{4,7},{5,4},{6,5},{7,6},{8,11},{9,8},{10,9... | collective-permute-start | bytes 1572872 | tf_op jit(solution)/shard_map/ppermute | solution.py:205
  261.4 31.0 %collective-permute-start.12 = (bf16[32,64,128]{2,1,0:T(8,128)(2,1)S(1)}, bf16[32,64,128]{2,1,0:T(8,128)(2,1)S(1)}, u32[]{:S(2)}, u32[]{:S(2)}) collective-permute-start(bf16[32,64,128]{2,1,0:T(8,128)(2,1)S(1)} %get-tuple-element.21.refs_4_), channel_id=1, source_target_pairs={{0,1},{1,2},{2,3},{3,0},{4,5},{5,6},{6,7},{7,4},{8,9},{9,10},{10,1... | collective-permute-start | bytes 1572872 | tf_op jit(solution)/shard_map/ppermute | solution.py:204
  272.1 20.3 %collective-permute-start.10 = (bf16[32,64,128]{2,1,0:T(8,128)(2,1)S(1)}, bf16[32,64,128]{2,1,0:T(8,128)(2,1)S(1)}, u32[]{:S(2)}, u32[]{:S(2)}) collective-permute-start(bf16[32,64,128]{2,1,0:T(8,128)(2,1)S(1)} %collective-permute-done.9.refs_1_), channel_id=1, source_target_pairs={{0,1},{1,2},{2,3},{3,0},{4,5},{5,6},{6,7},{7,4},{8,9},{9,10},{10,1... | collective-permute-start | bytes 1572872 | tf_op jit(solution)/shard_map/ppermute | solution.py:206
  272.2 20.2 %collective-permute-start.14 = (bf16[32,64,128]{2,1,0:T(8,128)(2,1)S(1)}, bf16[32,64,128]{2,1,0:T(8,128)(2,1)S(1)}, u32[]{:S(2)}, u32[]{:S(2)}) collective-permute-start(bf16[32,64,128]{2,1,0:T(8,128)(2,1)S(1)} %collective-permute-done.13.refs_7_), channel_id=1, source_target_pairs={{0,3},{1,0},{2,1},{3,2},{4,7},{5,4},{6,5},{7,6},{8,11},{9,8},{10,9... | collective-permute-start | bytes 1572872 | tf_op jit(solution)/shard_map/ppermute | solution.py:207
  (1 other events, 4.7 us)
Sparse Core Ops, SparseCore 0:
  9.8 90.8 all-gather.2

commit v2 on v1

v2 whole, which is shorter than its diff:
```python
import functools
import math

import jax
import jax.numpy as jnp
from jax import lax
from jax.experimental import pallas as pl
from jax.experimental.pallas import tpu as pltpu
from jax.sharding import PartitionSpec as P

PLACES = 4
LABEL_ROWS = 8
SPLIT = (80, 48)
VMEM_PRODUCTS = 54 * 1024 * 1024
VMEM_SUMS = 48 * 1024 * 1024
VMEM_BACK = 16 * 1024 * 1024


def product_kernel(
    row_block, owner, local, live, tiles, scaled, out, held, count, labels, arrived, *, first, rows, label
):
    groups, group, size, _ = held.shape

    def fetch(step):
        part = tiles.at[pl.ds(step * group, group)]
        return pltpu.make_async_copy(part, held.at[step], arrived.at[step])

    for step in range(groups):
        fetch(step).start()

    def clear(i, carry):
        count[i] = 0
        return carry

    lax.fori_loop(0, out.shape[0], clear, 0)
    if label:
        labels[...] = jnp.full(labels.shape, -1.0, labels.dtype)
    lane = lax.broadcasted_iota(jnp.int32, (LABEL_ROWS, size), 1)

    def multiply(step, carry):
        fetch(step).wait()
        for i in range(group):
            tile = step * group + i
            peer = owner[tile]
            place = count[peer]
            count[peer] = place + 1
            source = scaled[pl.ds(pl.multiple_of(row_block[tile] * size, size), size), :]
            product = lax.dot_general(
                held[step, i, :, first : first + rows],
                source,
                (((0,), (0,)), ((), ())),
                preferred_element_type=jnp.float32,
            )
            spot = pl.ds(pl.multiple_of(place * rows, rows), rows)
            out[peer, spot, :] = product.astype(out.dtype)
            if label:
                value = jnp.where(tile < live[0], local[tile], -1).astype(jnp.float32)
                old = labels[peer].astype(jnp.float32)
                labels[peer] = jnp.where(lane == place, value, old).astype(labels.dtype)
        return carry

    lax.fori_loop(0, groups, multiply, 0)
    if label:
        out[:, PLACES * rows :, :] = labels[...]


def products(row_block, owner, local, live, tiles, scaled, peers, first, rows, label):
    tile_count, size, _ = tiles.shape
    width = scaled.shape[1]
    group = 16
    groups = tile_count // group
    extra = LABEL_ROWS if label else 0
    scalars = [pl.BlockSpec(memory_space=pltpu.SMEM)] * 4
    return pl.pallas_call(
        functools.partial(product_kernel, first=first, rows=rows, label=label),
        in_specs=scalars
        + [pl.BlockSpec(memory_space=pltpu.HBM), pl.BlockSpec(memory_space=pltpu.VMEM)],
        out_specs=pl.BlockSpec(memory_space=pltpu.VMEM),
        scratch_shapes=[
            pltpu.VMEM((groups, group, size, size), jnp.bfloat16),
            pltpu.SMEM((peers,), jnp.int32),
            pltpu.VMEM((peers, LABEL_ROWS, width), jnp.bfloat16),
            pltpu.SemaphoreType.DMA((groups,)),
        ],
        out_shape=jax.ShapeDtypeStruct((peers, PLACES * rows + extra, width), jnp.bfloat16),
        compiler_params=pltpu.CompilerParams(vmem_limit_bytes=VMEM_PRODUCTS),
        cost_estimate=pl.CostEstimate(
            flops=2 * tile_count * size * rows * width,
            bytes_accessed=2 * tiles.size + 2 * scaled.size + 2 * peers * PLACES * rows * width,
            transcendentals=0,
        ),
        name="products",
    )(row_block, owner, local, live, tiles, scaled)


def sum_kernel(labels, incoming, scale, low, high, total, held, arrived, *, rows):
    half = low.shape[0]
    groups, group = held.shape[:2]

    def fetch(step):
        part = incoming.at[pl.ds(step * group, group)]
        return pltpu.make_async_copy(part, held.at[step], arrived.at[step])

    for step in range(groups):
        fetch(step).start()
    total[...] = jnp.zeros_like(total)

    def add(step, carry):
        fetch(step).wait()
        for i in range(group):
            for place in range(PLACES):
                block = labels[(step * group + i) * PLACES + place]
                slot = held[step, i, place * rows : (place + 1) * rows, :]
                total[block] += slot.astype(jnp.float32)
        return carry

    lax.fori_loop(0, groups, add, 0)
    low[...] = (total[:half] * scale[:half]).astype(low.dtype)
    high[...] = (total[half : 2 * half] * scale[half:]).astype(high.dtype)


def sums(labels, incoming, scale, rows):
    peers, depth, width = incoming.shape
    blocks = scale.shape[0]
    group = 8
    vmem = pl.BlockSpec(memory_space=pltpu.VMEM)
    return pl.pallas_call(
        functools.partial(sum_kernel, rows=rows),
        in_specs=[
            pl.BlockSpec(memory_space=pltpu.SMEM),
            pl.BlockSpec(memory_space=pltpu.HBM),
            vmem,
        ],
        out_specs=[vmem] * 2,
        scratch_shapes=[
            pltpu.VMEM((blocks + 1, rows, width), jnp.float32),
            pltpu.VMEM((peers // group, group, depth, width), jnp.bfloat16),
            pltpu.SemaphoreType.DMA((peers // group,)),
        ],
        out_shape=[jax.ShapeDtypeStruct((blocks // 2, rows, width), jnp.bfloat16)] * 2,
        compiler_params=pltpu.CompilerParams(vmem_limit_bytes=VMEM_SUMS),
        cost_estimate=pl.CostEstimate(
            flops=incoming.size,
            bytes_accessed=2 * incoming.size + 4 * scale.size + 2 * scale.size,
            transcendentals=0,
        ),
        name="sums",
    )(labels, incoming, scale)


def back_kernel(*refs, half, first, rows):
    low, high, (weight, features), out = refs[:4], refs[4:8], refs[8:10], refs[-1]
    group, width = features.shape[0], features.shape[2]

    def run(parts):
        whole = jnp.concatenate([part[...].reshape(group * rows, width) for part in parts], axis=1)
        back = lax.dot_general(
            whole, weight[...], (((1,), (0,)), ((), ())), preferred_element_type=jnp.float32
        ).reshape(group, rows, width)
        mask = features[:, first : first + rows, :].astype(jnp.float32) > 0
        out[:, first : first + rows, :] = jnp.where(mask, back, 0.0).astype(out.dtype)

    if first:
        out[:, :first, :] = refs[10][...]

    @pl.when(pl.program_id(0) < half)
    def _():
        run(low)

    @pl.when(pl.program_id(0) >= half)
    def _():
        run(high)


def back(low, high, weight, features, before, first, rows):
    blocks, size, width = features.shape
    steps = 4
    group = blocks // steps
    half = steps // 2
    specs = [pl.BlockSpec((group, rows, width), lambda i: (jnp.minimum(i, half - 1), 0, 0))] * 4
    specs += [pl.BlockSpec((group, rows, width), lambda i: (jnp.maximum(i - half, 0), 0, 0))] * 4
    specs += [
        pl.BlockSpec(weight.shape, lambda i: (0, 0)),
        pl.BlockSpec((group, size, width), lambda i: (i, 0, 0)),
    ]
    args = [*low, *high, weight, features]
    if first:
        specs.append(pl.BlockSpec((group, first, width), lambda i: (i, 0, 0)))
        args.append(before)
    return pl.pallas_call(
        functools.partial(back_kernel, half=half, first=first, rows=rows),
        grid=(steps,),
        in_specs=specs,
        out_specs=pl.BlockSpec((group, first + rows, width), lambda i: (i, 0, 0)),
        out_shape=jax.ShapeDtypeStruct((blocks, first + rows, width), jnp.bfloat16),
        compiler_params=pltpu.CompilerParams(vmem_limit_bytes=VMEM_BACK),
        cost_estimate=pl.CostEstimate(
            flops=2 * blocks * rows * width * weight.shape[0],
            bytes_accessed=2 * blocks * rows * (weight.shape[0] + 2 * width),
            transcendentals=0,
        ),
        name="back",
    )(*args)


def ring(shift, size):
    return [(i, (i + shift) % size) for i in range(size)]


def exchange(block):
    return lax.all_to_all(block, "row", split_axis=0, concat_axis=0, tiled=True)


def col_near(low, high):
    ahead, behind = ring(1, lax.axis_size("col")), ring(-1, lax.axis_size("col"))
    low_left = lax.ppermute(low, "col", ahead)
    high_right = lax.ppermute(high, "col", behind)
    high_left = lax.ppermute(high, "col", ahead)
    low_right = lax.ppermute(low, "col", behind)
    return low_left, high_left, low_right, high_right


def col_far(low_left, high_right):
    size = lax.axis_size("col")
    return (
        lax.ppermute(low_left, "col", ring(1, size)),
        lax.ppermute(high_right, "col", ring(-1, size)),
    )


def pair_up(own, near, far):
    low = (own[0], near[0], far[0], near[2])
    high = (own[1], near[1], far[1], near[3])
    return low, high


def weight_rows(weight):
    size = lax.axis_size("col")
    width = weight.shape[1]
    me = lax.axis_index("col")
    parts = []
    for shift in range(size):
        start = lax.rem(me + shift, size) * width
        slab = lax.dynamic_slice_in_dim(weight, start, width, 0)
        parts.append(slab if shift == 0 else lax.ppermute(slab, "col", ring(shift, size)))
    return jnp.concatenate(parts, axis=1).T


def per_device(
    grad_out, features, weight, tiles, tile_row_block, tile_owner, tile_local, degrees, live
):
    node_rows, width = grad_out.shape
    size = tiles.shape[1]
    blocks = node_rows // size
    peers = lax.axis_size("row")
    cols = lax.axis_size("col")
    scale = lax.rsqrt(degrees.astype(jnp.float32))
    scaled = (grad_out.astype(jnp.float32) * scale[:, None]).astype(jnp.bfloat16)
    owner = tile_owner[:, 0]
    weight_mine = weight_rows(weight)
    blocked = features.reshape(blocks, size, width)
    wide_scale = jnp.broadcast_to(scale.reshape(blocks, size, 1), (blocks, size, width))

    starts = [sum(SPLIT[:k]) for k in range(len(SPLIT))]
    gathered = lax.all_gather(features, "col", axis=0).reshape(cols, blocks, size, width)
    outgoing = [
        products(tile_row_block, owner, tile_local, live, tiles, scaled, peers, first, rows, k == 0)
        for k, (first, rows) in enumerate(zip(starts, SPLIT))
    ]
    outgoing[1], weight_mine, gathered = lax.optimization_barrier(
        (outgoing[1], weight_mine, gathered)
    )
    incoming = [exchange(each) for each in outgoing]

    tags = incoming[0][:, PLACES * SPLIT[0], :PLACES].astype(jnp.int32).reshape(-1)
    tags = jnp.where(tags < 0, blocks, tags)
    scales = [wide_scale[:, first : first + rows] for first, rows in zip(starts, SPLIT)]

    def local_terms(own, first, rows):
        return lax.dot_general(
            gathered[:, :, first : first + rows],
            jnp.concatenate(own, axis=0),
            (((1, 2), (0, 1)), ((), ())),
            preferred_element_type=jnp.float32,
        )

    own = sums(tags, incoming[0], scales[0], SPLIT[0])
    near = col_near(*own)
    far = col_far(near[0], near[3])
    terms = local_terms(own, 0, SPLIT[0])
    before = back(*pair_up(own, near, far), weight_mine, blocked, None, 0, SPLIT[0])
    incoming[1], scales[1], terms, before = lax.optimization_barrier(
        (incoming[1], scales[1], terms, before)
    )

    own = sums(tags, incoming[1], scales[1], SPLIT[1])
    near = col_near(*own)
    terms = terms + local_terms(own, *SPLIT)
    norm_factor = 1.0 / math.sqrt(node_rows * peers)
    share = cols * width // peers
    total = jnp.sum(exchange(terms.reshape(peers, share, width)), axis=0) * norm_factor
    total = jnp.broadcast_to(total.astype(jnp.bfloat16)[None], (peers, share, width))
    near, _ = lax.optimization_barrier((near, total))
    far = col_far(near[0], near[3])
    grad_pre = back(*pair_up(own, near, far), weight_mine, blocked, before, *SPLIT)
    grad_weight = exchange(total).astype(jnp.float32)
    return (grad_pre.reshape(node_rows, width), grad_weight.reshape(cols * width, width))


def solution(mesh):
    return jax.shard_map(
        per_device,
        mesh=mesh,
        in_specs=(
            P("row", "col"),
            P("row", "col"),
            P(None, "col"),
            P("row", None, None),
            P("row"),
            P("row", None),
            P("row"),
            P("row"),
            P("row"),
        ),
        out_specs=(P("row", "col"), P(None, "col")),
        check_vma=False,
    )
```

time: 305 us -> 296 us (0.970)
  blocking collectives: 16.8 us -> 0 us
  Pallas kernels: 45.8 us -> 34.1 us
  starting transfers between devices: 43.5 us -> 50.7 us
  local copies, waits for them, and re-layouts: 1.88 us -> 5.91 us
  waiting for transfers between devices: 170 us -> 174 us
  matrix products: 4.78 us -> 8.02 us
    all_to_all x1 -> x0, blocking collectives: 16.8 us -> none  [exchange(): return lax.all_to_all(block, 'row', split_axis=0, concat_axis=0, tiled=True)]
    ppermute x12, waiting for transfers between devices: 29.9 us -> 37.9 us  [the longest x2 13.9 us: col_far(): lax.ppermute(low_left, 'col', ring(1, size))]
    all_to_all x3 -> x4, waiting for transfers between devices: 93.2 us -> 85.8 us  [exchange(): return lax.all_to_all(block, 'row', split_axis=0, concat_axis=0, tiled=True)]
    pallas_call x4, Pallas kernels: 21 us -> 13.6 us  [the longest x2 6.9 us: back(): pl.pallas_call(functools.partial(back_kernel, half=half, first=first, row...]
    all_to_all x3 -> x4, starting transfers between devices: 25.7 us -> 31.8 us  [exchange(): return lax.all_to_all(block, 'row', split_axis=0, concat_axis=0, tiled=True)]
    pallas_call x2, Pallas kernels: 24.8 us -> 20.5 us  [products(): pl.pallas_call(functools.partial(product_kernel, first=first, rows=rows,...]
    all_gather x1, waiting for transfers between devices: 46.2 us -> 49.6 us  [per_device(): lax.all_gather(features, 'col', axis=0).reshape(cols, blocks, size, width)]
    dot_general x2, matrix products: 4.78 us -> 8.02 us  [local_terms(): lax.dot_general(gathered[:, :, first:first + rows], jnp.concatenate(own,...]
  transfers between devices with their start and end apart: 19 -> 20, of which waited for: 8 -> 10; matrix products, arithmetic and copies ran while one was open for 4% -> 5% of each run, Pallas kernels for 12% -> 9%
where the time goes in v2:
time: 296 us; the launch traced here: 295 us
  waiting for transfers between devices  174 us (59%)
  starting transfers between devices  50.7 us (17%)
  Pallas kernels  34.1 us (12%)
  between operations  15 us (5%)
  matrix products  8.02 us (3%)
  other arithmetic  7.39 us (2%)
  local copies, waits for them, and re-layouts  5.91 us (2%)
    all_to_all x4, waiting for transfers between devices, exchange(): return lax.all_to_all(block, 'row', split_axis=0, concat_axis=0, tiled=True)  85.8 us
    all_gather x1, waiting for transfers between devices, per_device(): lax.all_gather(features, 'col', axis=0).reshape(cols, blocks, size, width)  49.6 us
    all_to_all x4, starting transfers between devices, exchange(): return lax.all_to_all(block, 'row', split_axis=0, concat_axis=0, tiled=True)  31.8 us
    pallas_call x2, Pallas kernels, products(): pl.pallas_call(functools.partial(product_kernel, first=first, rows=rows,...  20.5 us
    ppermute x2, waiting for transfers between devices, col_far(): lax.ppermute(low_left, 'col', ring(1, size))  13.9 us
    ppermute x2, waiting for transfers between devices, col_near(): low_left = lax.ppermute(low, 'col', ahead)  13.3 us
    ppermute x2, waiting for transfers between devices, col_near(): low_right = lax.ppermute(low, 'col', behind)  10.3 us
    dot_general x2, matrix products, local_terms(): lax.dot_general(gathered[:, :, first:first + rows], jnp.concatenate(own,...  8.02 us
  transfers between devices with their start and end apart: 20, of which 10 were waited for; matrix products, arithmetic and copies ran while one was open for 5% of the time, Pallas kernels for 9%

profile of v2, /device:TPU:1, one launch (start us, length us, event | category | flops | bytes accessed | tf_op | source)
XLA Modules:
  0.0 295.1 jit_solution(15942077444960758435)
XLA Ops:
  9.3 2.2 multiply_convert_fusion.scaled
  11.6 9.5 %products.2 = bf16[64,328,128]{2,1,0:T(8,128)(2,1)} custom-call(s32[192]{0:T(256)} %row_block.3, s32[192]{0:T(256)} %bitcast.32, s32[192]{0:T(256)} %local.3, s32[1]{0:T(128)S(6)} %copy.32.live, bf16[192,128,128]{2,1,0:T(8,128)(2,1)} %tiles.3, bf16[8192,128]{1,0:T(8,128)(2,1)} %multiply_convert_fusion.scaled), custom_call_target="tpu_custom_call" | custom-call | flops 503316480 | bytes 13631488 | tf_op jit(solution)/shard_map/products/pallas_call | solution.py:74
  21.1 13.5 %all-to-all-start = ((bf16[64,328,128]{2,1,0:T(8,128)(2,1)}), bf16[64,328,128]{2,1,0:T(8,128)(2,1)}, u32[]{:S(2)}, u32[]{:S(2)}) async-start(bf16[64,328,128]{2,1,0:T(8,128)(2,1)} %products.2), calls=%async_computation | async-start | bytes 10747904 | tf_op jit(solution)/shard_map/all_to_all | solution.py:211
  36.1 2.5 collective-permute-start.1
  40.1 11.0 %products.3 = bf16[64,192,128]{2,1,0:T(8,128)(2,1)} custom-call(s32[192]{0:T(256)} %row_block.3, s32[192]{0:T(256)} %bitcast.33, s32[192]{0:T(256)} %local.3, s32[1]{0:T(128)S(6)} %copy.32.live, bf16[192,128,128]{2,1,0:T(8,128)(2,1)} %tiles.3, bf16[8192,128]{1,0:T(8,128)(2,1)} %multiply_convert_fusion.scaled), custom_call_target="tpu_custom_call" | custom-call | flops 301989888 | bytes 11534336 | tf_op jit(solution)/shard_map/products/pallas_call | solution.py:74
  51.1 49.6 %all-gather.3.cloned.1.call-done = bf16[32768,128]{1,0:T(8,128)(2,1)} async-done(((bf16[8192,128]{1,0:T(8,128)(2,1)}), bf16[32768,128]{1,0:T(8,128)(2,1)}) %all-gather.3.cloned.1.call-update) | async-done | bytes 8388624 | tf_op jit(solution)/shard_map/all_gather | solution.py:265
  100.7 55.0 %all-to-all-done.incoming = bf16[64,328,128]{2,1,0:T(8,128)(2,1)} async-done(((bf16[64,328,128]{2,1,0:T(8,128)(2,1)}), bf16[64,328,128]{2,1,0:T(8,128)(2,1)}, u32[]{:S(2)}, u32[]{:S(2)}) %all-to-all-start) | async-done | bytes 5373984 | tf_op jit(solution)/shard_map/all_to_all | solution.py:211
  155.8 6.0 %all-to-all-start.1 = ((bf16[64,192,128]{2,1,0:T(8,128)(2,1)}), bf16[64,192,128]{2,1,0:T(8,128)(2,1)}, u32[]{:S(2)}, u32[]{:S(2)}) async-start(bf16[64,192,128]{2,1,0:T(8,128)(2,1)} %products.3), calls=%async_computation.1 | async-start | bytes 6291456 | tf_op jit(solution)/shard_map/all_to_all | solution.py:211
  163.6 3.6 %sums.2 = (bf16[32,80,128]{2,1,0:T(8,128)(2,1)S(1)}, bf16[32,80,128]{2,1,0:T(8,128)(2,1)S(1)}) custom-call(s32[256]{0:T(256)S(1)} %compare_select_fusion.labels, bf16[64,328,128]{2,1,0:T(8,128)(2,1)} %all-to-all-done.incoming, f32[64,80,128]{2,1,0:T(8,128)S(1)} %broadcast_in_dim.23.scale), custom_call_target="tpu_custom_call" | custom-call | flops 2686976 | bytes 9306112 | tf_op jit(solution)/shard_map/sums/pallas_call | solution.py:127
  171.5 13.0 %collective-permute-done.3.refs_1_ = bf16[32,80,128]{2,1,0:T(8,128)(2,1)S(1)} collective-permute-done((bf16[32,80,128]{2,1,0:T(8,128)(2,1)S(1)}, bf16[32,80,128]{2,1,0:T(8,128)(2,1)S(1)}, u32[]{:S(2)}, u32[]{:S(2)}) %collective-permute-start.3) | collective-permute-done | bytes 655392 | tf_op jit(solution)/shard_map/ppermute | solution.py:216
  184.4 2.7 collective-permute-start.8
  187.8 10.3 %collective-permute-done.5.refs_3_ = bf16[32,80,128]{2,1,0:T(8,128)(2,1)S(1)} collective-permute-done((bf16[32,80,128]{2,1,0:T(8,128)(2,1)S(1)}, bf16[32,80,128]{2,1,0:T(8,128)(2,1)S(1)}, u32[]{:S(2)}, u32[]{:S(2)}) %collective-permute-start.5) | collective-permute-done | bytes 655392 | tf_op jit(solution)/shard_map/ppermute | solution.py:219
  198.5 13.9 %collective-permute-done.4.refs_2_ = bf16[32,80,128]{2,1,0:T(8,128)(2,1)S(1)} collective-permute-done((bf16[32,80,128]{2,1,0:T(8,128)(2,1)S(1)}, bf16[32,80,128]{2,1,0:T(8,128)(2,1)S(1)}, u32[]{:S(2)}, u32[]{:S(2)}) %collective-permute-start.4) | collective-permute-done | bytes 655392 | tf_op jit(solution)/shard_map/ppermute | solution.py:226
  212.4 2.1 back.2.refs_10_
  214.5 4.8 %fusion.6 = f32[4,128,128]{2,1,0:T(8,128)} fusion(bf16[32,80,128]{2,1,0:T(8,128)(2,1)S(1)} %get-tuple-element.20.refs_4_, bf16[32,80,128]{2,1,0:T(8,128)(2,1)S(1)} %get-tuple-element.19.refs_0_, bf16[4,64,128,128]{3,2,1,0:T(8,128)(2,1)} %bitcast.34), kind=kOutput, calls=%fused_computation.8 | convolution fusion | flops 671744000 | bytes 6815744 | tf_op jit(solution)/shard_map/dot_general | solution.py:280
  219.3 15.9 %all-to-all-done.1.incoming = bf16[64,192,128]{2,1,0:T(8,128)(2,1)} async-done(((bf16[64,192,128]{2,1,0:T(8,128)(2,1)}), bf16[64,192,128]{2,1,0:T(8,128)(2,1)}, u32[]{:S(2)}, u32[]{:S(2)}) %all-to-all-start.1) | async-done | bytes 3145760 | tf_op jit(solution)/shard_map/all_to_all | solution.py:211
  236.4 3.1 %sums.3 = (bf16[32,48,128]{2,1,0:T(8,128)(2,1)S(1)}, bf16[32,48,128]{2,1,0:T(8,128)(2,1)S(1)}) custom-call(s32[256]{0:T(256)S(1)} %compare_select_fusion.labels, bf16[64,192,128]{2,1,0:T(8,128)(2,1)} %all-to-all-done.1.incoming, f32[64,48,128]{2,1,0:T(8,128)S(1)} %broadcast_in_dim.22.scale), custom_call_target="tpu_custom_call" | custom-call | flops 1572864 | bytes 5505024 | tf_op jit(solution)/shard_map/sums/pallas_call | solution.py:127
  239.5 3.2 %fusion.9 = f32[4,128,128]{2,1,0:T(8,128)S(1)} fusion(bf16[4,64,128,128]{3,2,1,0:T(8,128)(2,1)} %bitcast.35, bf16[32,48,128]{2,1,0:T(8,128)(2,1)S(1)} %get-tuple-element.25.refs_4_, bf16[32,48,128]{2,1,0:T(8,128)(2,1)S(1)} %get-tuple-element.24.refs_0_), kind=kOutput, calls=%fused_computation.9 | convolution fusion | flops 403046400 | bytes 4194304 | tf_op jit(solution)/shard_map/dot_general | solution.py:280
  243.5 6.2 %all-to-all-start.2 = ((f32[64,8,128]{2,1,0:T(8,128)}), f32[64,8,128]{2,1,0:T(8,128)}, u32[]{:S(2)}, u32[]{:S(2)}) async-start(f32[64,8,128]{2,1,0:T(8,128)} %bitcast.30), calls=%async_computation.2 | async-start | bytes 524288 | tf_op jit(solution)/shard_map/all_to_all | solution.py:211
  253.9 7.7 %all-to-all-done.2 = f32[64,8,128]{2,1,0:T(8,128)} async-done(((f32[64,8,128]{2,1,0:T(8,128)}), f32[64,8,128]{2,1,0:T(8,128)}, u32[]{:S(2)}, u32[]{:S(2)}) %all-to-all-start.2) | async-done | bytes 262176 | tf_op jit(solution)/shard_map/all_to_all | solution.py:211
  263.3 6.2 %all-to-all-start.3 = ((bf16[64,8,128]{2,1,0:T(8,128)(2,1)}), bf16[64,8,128]{2,1,0:T(8,128)(2,1)}, u32[]{:S(2)}, u32[]{:S(2)}) async-start(bf16[64,8,128]{2,1,0:T(8,128)(2,1)} %broadcast_in_dim.24), calls=%async_computation.3 | async-start | bytes 262144 | tf_op jit(solution)/shard_map/all_to_all | solution.py:211
  270.9 1.7 collective-permute-start.14
  272.6 7.3 %all-to-all-done.3 = bf16[64,8,128]{2,1,0:T(8,128)(2,1)} async-done(((bf16[64,8,128]{2,1,0:T(8,128)(2,1)}), bf16[64,8,128]{2,1,0:T(8,128)(2,1)}, u32[]{:S(2)}, u32[]{:S(2)}) %all-to-all-start.3) | async-done | bytes 131104 | tf_op jit(solution)/shard_map/all_to_all | solution.py:211
  283.5 4.8 %back.3 = bf16[64,128,128]{2,1,0:T(8,128)(2,1)} custom-call(bf16[32,48,128]{2,1,0:T(8,128)(2,1)S(1)} %copy-done.2, bf16[32,48,128]{2,1,0:T(8,128)(2,1)} %collective-permute-done.9.refs_1_, bf16[32,48,128]{2,1,0:T(8,128)(2,1)} %collective-permute-done.13.refs_2_, bf16[32,48,128]{2,1,0:T(8,128)(2,1)} %collective-permute-done.11.refs_3_, ...), custom_call_target="tpu_custom_call" | custom-call | flops 402653184 | bytes 4718592 | tf_op jit(solution)/shard_map/back/pallas_call | solution.py:190
  (60 shorter events, 24.4 us)
Async XLA Ops:
  7.2 93.5 %all-gather.3.cloned.1.call-start = ((), (), s32[]{:S(2)}) async-start(), calls=%async_computation.4 | async-start | bytes 10485760 | tf_op jit(solution)/shard_map/all_gather | solution.py:265
  21.1 13.5 %copy-start.7 = (bf16[512,128]{1,0:T(8,128)(2,1)S(1)}, bf16[512,128]{1,0:T(8,128)(2,1)}, u32[]{:S(2)}) copy-start(bf16[512,128]{1,0:T(8,128)(2,1)} %param.11) | copy-start | bytes 393220
  21.1 134.7 %all-to-all-start = ((bf16[64,328,128]{2,1,0:T(8,128)(2,1)}), bf16[64,328,128]{2,1,0:T(8,128)(2,1)}, u32[]{:S(2)}, u32[]{:S(2)}) async-start(bf16[64,328,128]{2,1,0:T(8,128)(2,1)} %products.2), calls=%async_computation | async-start | bytes 10747904 | tf_op jit(solution)/shard_map/all_to_all | solution.py:211
  34.7 16.4 %collective-permute-start = (bf16[128,128]{0,1:T(8,128)(2,1)S(1)}, bf16[128,128]{0,1:T(8,128)(2,1)S(1)}, u32[]{:S(2)}, u32[]{:S(2)}) collective-permute-start(bf16[128,128]{0,1:T(8,128)(2,1)S(1)} %copy.29), channel_id=1, source_target_pairs={{0,1},{1,2},{2,3},{3,0},{4,5},{5,6},{6,7},{7,4},{8,9},{9,10},{10,1... | collective-permute-start | bytes 98312 | tf_op jit(solution)/shard_map/ppermute | solution.py:245
  36.1 15.0 %collective-permute-start.1 = (bf16[128,128]{0,1:T(8,128)(2,1)S(1)}, bf16[128,128]{0,1:T(8,128)(2,1)S(1)}, u32[]{:S(2)}, u32[]{:S(2)}) collective-permute-start(bf16[128,128]{0,1:T(8,128)(2,1)S(1)} %copy.30), channel_id=1, source_target_pairs={{0,2},{1,3},{2,0},{3,1},{4,6},{5,7},{6,4},{7,5},{8,10},{9,11},{10,... | collective-permute-start | bytes 98312 | tf_op jit(solution)/shard_map/ppermute | solution.py:245
  38.8 12.3 %collective-permute-start.2 = (bf16[128,128]{0,1:T(8,128)(2,1)S(1)}, bf16[128,128]{0,1:T(8,128)(2,1)S(1)}, u32[]{:S(2)}, u32[]{:S(2)}) collective-permute-start(bf16[128,128]{0,1:T(8,128)(2,1)S(1)} %copy.31), channel_id=1, source_target_pairs={{0,3},{1,0},{2,1},{3,2},{4,7},{5,4},{6,5},{7,6},{8,11},{9,8},{10,9... | collective-permute-start | bytes 98312 | tf_op jit(solution)/shard_map/ppermute | solution.py:245
  155.8 79.4 %all-to-all-start.1 = ((bf16[64,192,128]{2,1,0:T(8,128)(2,1)}), bf16[64,192,128]{2,1,0:T(8,128)(2,1)}, u32[]{:S(2)}, u32[]{:S(2)}) async-start(bf16[64,192,128]{2,1,0:T(8,128)(2,1)} %products.3), calls=%async_computation.1 | async-start | bytes 6291456 | tf_op jit(solution)/shard_map/all_to_all | solution.py:211
  163.6 48.8 %copy-start = (bf16[8192,128]{1,0:T(8,128)(2,1)S(1)}, bf16[8192,128]{1,0:T(8,128)(2,1)}, u32[]{:S(2)}) copy-start(bf16[8192,128]{1,0:T(8,128)(2,1)} %param.10) | copy-start | bytes 6291460
  167.2 17.2 %collective-permute-start.3 = (bf16[32,80,128]{2,1,0:T(8,128)(2,1)S(1)}, bf16[32,80,128]{2,1,0:T(8,128)(2,1)S(1)}, u32[]{:S(2)}, u32[]{:S(2)}) collective-permute-start(bf16[32,80,128]{2,1,0:T(8,128)(2,1)S(1)} %get-tuple-element.19.refs_0_), channel_id=1, source_target_pairs={{0,1},{1,2},{2,3},{3,0},{4,5},{5,6},{6,7},{7,4},{8,9},{9,10},{10,1... | collective-permute-start | bytes 1966088 | tf_op jit(solution)/shard_map/ppermute | solution.py:216
  168.5 15.9 %collective-permute-start.7 = (bf16[32,80,128]{2,1,0:T(8,128)(2,1)S(1)}, bf16[32,80,128]{2,1,0:T(8,128)(2,1)S(1)}, u32[]{:S(2)}, u32[]{:S(2)}) collective-permute-start(bf16[32,80,128]{2,1,0:T(8,128)(2,1)S(1)} %get-tuple-element.20.refs_4_), channel_id=1, source_target_pairs={{0,3},{1,0},{2,1},{3,2},{4,7},{5,4},{6,5},{7,6},{8,11},{9,8},{10,9... | collective-permute-start | bytes 1966088 | tf_op jit(solution)/shard_map/ppermute | solution.py:217
  170.0 28.2 %collective-permute-start.5 = (bf16[32,80,128]{2,1,0:T(8,128)(2,1)S(1)}, bf16[32,80,128]{2,1,0:T(8,128)(2,1)S(1)}, u32[]{:S(2)}, u32[]{:S(2)}) collective-permute-start(bf16[32,80,128]{2,1,0:T(8,128)(2,1)S(1)} %get-tuple-element.19.refs_0_), channel_id=1, source_target_pairs={{0,3},{1,0},{2,1},{3,2},{4,7},{5,4},{6,5},{7,6},{8,11},{9,8},{10,9... | collective-permute-start | bytes 1966088 | tf_op jit(solution)/shard_map/ppermute | solution.py:219
  171.3 27.2 %collective-permute-start.6 = (bf16[32,80,128]{2,1,0:T(8,128)(2,1)S(1)}, bf16[32,80,128]{2,1,0:T(8,128)(2,1)S(1)}, u32[]{:S(2)}, u32[]{:S(2)}) collective-permute-start(bf16[32,80,128]{2,1,0:T(8,128)(2,1)S(1)} %get-tuple-element.20.refs_4_), channel_id=1, source_target_pairs={{0,1},{1,2},{2,3},{3,0},{4,5},{5,6},{6,7},{7,4},{8,9},{9,10},{10,1... | collective-permute-start | bytes 1966088 | tf_op jit(solution)/shard_map/ppermute | solution.py:218
  184.4 28.0 %collective-permute-start.4 = (bf16[32,80,128]{2,1,0:T(8,128)(2,1)S(1)}, bf16[32,80,128]{2,1,0:T(8,128)(2,1)S(1)}, u32[]{:S(2)}, u32[]{:S(2)}) collective-permute-start(bf16[32,80,128]{2,1,0:T(8,128)(2,1)S(1)} %collective-permute-done.3.refs_1_), channel_id=1, source_target_pairs={{0,1},{1,2},{2,3},{3,0},{4,5},{5,6},{6,7},{7,4},{8,9},{9,10},{10,1... | collective-permute-start | bytes 1966088 | tf_op jit(solution)/shard_map/ppermute | solution.py:226
  184.4 28.0 %collective-permute-start.8 = (bf16[32,80,128]{2,1,0:T(8,128)(2,1)S(1)}, bf16[32,80,128]{2,1,0:T(8,128)(2,1)S(1)}, u32[]{:S(2)}, u32[]{:S(2)}) collective-permute-start(bf16[32,80,128]{2,1,0:T(8,128)(2,1)S(1)} %collective-permute-done.7.refs_7_), channel_id=1, source_target_pairs={{0,3},{1,0},{2,1},{3,2},{4,7},{5,4},{6,5},{7,6},{8,11},{9,8},{10,9... | collective-permute-start | bytes 1966088 | tf_op jit(solution)/shard_map/ppermute | solution.py:227
  239.5 3.3 %copy-start.1 = (bf16[32,48,128]{2,1,0:T(8,128)(2,1)}, bf16[32,48,128]{2,1,0:T(8,128)(2,1)S(1)}, u32[]{:S(2)}) copy-start(bf16[32,48,128]{2,1,0:T(8,128)(2,1)S(1)} %get-tuple-element.24.refs_0_) | copy-start | bytes 1179652
  239.5 3.3 %copy-start.3 = (bf16[32,48,128]{2,1,0:T(8,128)(2,1)}, bf16[32,48,128]{2,1,0:T(8,128)(2,1)S(1)}, u32[]{:S(2)}) copy-start(bf16[32,48,128]{2,1,0:T(8,128)(2,1)S(1)} %get-tuple-element.25.refs_4_) | copy-start | bytes 1179652
  243.5 18.1 %all-to-all-start.2 = ((f32[64,8,128]{2,1,0:T(8,128)}), f32[64,8,128]{2,1,0:T(8,128)}, u32[]{:S(2)}, u32[]{:S(2)}) async-start(f32[64,8,128]{2,1,0:T(8,128)} %bitcast.30), calls=%async_computation.2 | async-start | bytes 524288 | tf_op jit(solution)/shard_map/all_to_all | solution.py:211
  249.7 19.8 %collective-permute-start.10 = (bf16[32,48,128]{2,1,0:T(8,128)(2,1)}, bf16[32,48,128]{2,1,0:T(8,128)(2,1)}, u32[]{:S(2)}, u32[]{:S(2)}) collective-permute-start(bf16[32,48,128]{2,1,0:T(8,128)(2,1)} %copy-done.3), channel_id=1, source_target_pairs={{0,1},{1,2},{2,3},{3,0},{4,5},{5,6},{6,7},{7,4},{8,9},{9,10},{10,1... | collective-permute-start | bytes 1179656 | tf_op jit(solution)/shard_map/ppermute | solution.py:218
  251.0 18.6 %collective-permute-start.11 = (bf16[32,48,128]{2,1,0:T(8,128)(2,1)}, bf16[32,48,128]{2,1,0:T(8,128)(2,1)}, u32[]{:S(2)}, u32[]{:S(2)}) collective-permute-start(bf16[32,48,128]{2,1,0:T(8,128)(2,1)} %copy-done.1), channel_id=1, source_target_pairs={{0,3},{1,0},{2,1},{3,2},{4,7},{5,4},{6,5},{7,6},{8,11},{9,8},{10,9... | collective-permute-start | bytes 1179656 | tf_op jit(solution)/shard_map/ppermute | solution.py:219
  252.5 17.1 %collective-permute-start.12 = (bf16[32,48,128]{2,1,0:T(8,128)(2,1)}, bf16[32,48,128]{2,1,0:T(8,128)(2,1)}, u32[]{:S(2)}, u32[]{:S(2)}) collective-permute-start(bf16[32,48,128]{2,1,0:T(8,128)(2,1)} %copy-done.3), channel_id=1, source_target_pairs={{0,3},{1,0},{2,1},{3,2},{4,7},{5,4},{6,5},{7,6},{8,11},{9,8},{10,9... | collective-permute-start | bytes 1179656 | tf_op jit(solution)/shard_map/ppermute | solution.py:217
  253.7 16.2 %collective-permute-start.9 = (bf16[32,48,128]{2,1,0:T(8,128)(2,1)}, bf16[32,48,128]{2,1,0:T(8,128)(2,1)}, u32[]{:S(2)}, u32[]{:S(2)}) collective-permute-start(bf16[32,48,128]{2,1,0:T(8,128)(2,1)} %copy-done.1), channel_id=1, source_target_pairs={{0,1},{1,2},{2,3},{3,0},{4,5},{5,6},{6,7},{7,4},{8,9},{9,10},{10,1... | collective-permute-start | bytes 1179656 | tf_op jit(solution)/shard_map/ppermute | solution.py:216
  263.3 16.5 %all-to-all-start.3 = ((bf16[64,8,128]{2,1,0:T(8,128)(2,1)}), bf16[64,8,128]{2,1,0:T(8,128)(2,1)}, u32[]{:S(2)}, u32[]{:S(2)}) async-start(bf16[64,8,128]{2,1,0:T(8,128)(2,1)} %broadcast_in_dim.24), calls=%async_computation.3 | async-start | bytes 262144 | tf_op jit(solution)/shard_map/all_to_all | solution.py:211
  269.9 11.6 %collective-permute-start.13 = (bf16[32,48,128]{2,1,0:T(8,128)(2,1)}, bf16[32,48,128]{2,1,0:T(8,128)(2,1)}, u32[]{:S(2)}, u32[]{:S(2)}) collective-permute-start(bf16[32,48,128]{2,1,0:T(8,128)(2,1)} %collective-permute-done.9.refs_1_), channel_id=1, source_target_pairs={{0,1},{1,2},{2,3},{3,0},{4,5},{5,6},{6,7},{7,4},{8,9},{9,10},{10,1... | collective-permute-start | bytes 1179656 | tf_op jit(solution)/shard_map/ppermute | solution.py:226
  270.9 10.6 %collective-permute-start.14 = (bf16[32,48,128]{2,1,0:T(8,128)(2,1)}, bf16[32,48,128]{2,1,0:T(8,128)(2,1)}, u32[]{:S(2)}, u32[]{:S(2)}) collective-permute-start(bf16[32,48,128]{2,1,0:T(8,128)(2,1)} %collective-permute-done.12.refs_7_), channel_id=1, source_target_pairs={{0,3},{1,0},{2,1},{3,2},{4,7},{5,4},{6,5},{7,6},{8,11},{9,8},{10,9... | collective-permute-start | bytes 1179656 | tf_op jit(solution)/shard_map/ppermute | solution.py:227
  (4 other events, 7.4 us)
Sparse Core Ops, SparseCore 0:
  9.8 90.8 all-gather.2

commit v3 on v2

--- a/solution.py
+++ b/solution.py
@@ -10,6 +10,7 @@
 
 PLACES = 4
 LABEL_ROWS = 8
+STRIP = 16
 SPLIT = (80, 48)
 VMEM_PRODUCTS = 54 * 1024 * 1024
 VMEM_SUMS = 48 * 1024 * 1024
@@ -93,7 +94,7 @@
     )(row_block, owner, local, live, tiles, scaled)
 
 
-def sum_kernel(labels, incoming, scale, low, high, total, held, arrived, *, rows):
+def sum_kernel(labels, incoming, scale, low, high, total, held, wide, arrived, *, rows):
     half = low.shape[0]
     groups, group = held.shape[:2]
 
@@ -104,6 +105,19 @@
     for step in range(groups):
         fetch(step).start()
     total[...] = jnp.zeros_like(total)
+    own_lane = lax.broadcasted_iota(jnp.int32, (rows, rows), 0) == lax.broadcasted_iota(
+        jnp.int32, (rows, rows), 1
+    )
+
+    def widen(i, carry):
+        for j in range(4):
+            block = i * 4 + j
+            row = scale[pl.ds(block, 1), :]
+            column = jnp.sum(jnp.where(own_lane, row, 0.0), axis=1, keepdims=True)
+            wide[block] = jnp.broadcast_to(column, wide.shape[1:])
+        return carry
+
+    lax.fori_loop(0, wide.shape[0] // 4, widen, 0)
 
     def add(step, carry):
         fetch(step).wait()
@@ -115,8 +129,8 @@
         return carry
 
     lax.fori_loop(0, groups, add, 0)
-    low[...] = (total[:half] * scale[:half]).astype(low.dtype)
-    high[...] = (total[half : 2 * half] * scale[half:]).astype(high.dtype)
+    low[...] = (total[:half] * wide[:half]).astype(low.dtype)
+    high[...] = (total[half : 2 * half] * wide[half:]).astype(high.dtype)
 
 
 def sums(labels, incoming, scale, rows):
@@ -135,64 +149,63 @@
         scratch_shapes=[
             pltpu.VMEM((blocks + 1, rows, width), jnp.float32),
             pltpu.VMEM((peers // group, group, depth, width), jnp.bfloat16),
+            pltpu.VMEM((blocks, rows, width), jnp.float32),
             pltpu.SemaphoreType.DMA((peers // group,)),
         ],
         out_shape=[jax.ShapeDtypeStruct((blocks // 2, rows, width), jnp.bfloat16)] * 2,
         compiler_params=pltpu.CompilerParams(vmem_limit_bytes=VMEM_SUMS),
         cost_estimate=pl.CostEstimate(
             flops=incoming.size,
-            bytes_accessed=2 * incoming.size + 4 * scale.size + 2 * scale.size,
+            bytes_accessed=2 * incoming.size + 2 * scale.size * width,
             transcendentals=0,
         ),
         name="sums",
     )(labels, incoming, scale)
 
 
-def back_kernel(*refs, half, first, rows):
+def back_kernel(*refs):
     low, high, (weight, features), out = refs[:4], refs[4:8], refs[8:10], refs[-1]
-    group, width = features.shape[0], features.shape[2]
+    half, _, strip, width = features.shape
 
     def run(parts):
-        whole = jnp.concatenate([part[...].reshape(group * rows, width) for part in parts], axis=1)
+        whole = jnp.concatenate([part[...].reshape(half * strip, width) for part in parts], axis=1)
         back = lax.dot_general(
             whole, weight[...], (((1,), (0,)), ((), ())), preferred_element_type=jnp.float32
-        ).reshape(group, rows, width)
-        mask = features[:, first : first + rows, :].astype(jnp.float32) > 0
-        out[:, first : first + rows, :] = jnp.where(mask, back, 0.0).astype(out.dtype)
-
-    if first:
-        out[:, :first, :] = refs[10][...]
-
-    @pl.when(pl.program_id(0) < half)
+        ).reshape(features.shape)
+        mask = features[...].astype(jnp.float32) > 0
+        out[...] = jnp.where(mask, back, 0.0).astype(out.dtype)
+
+    @pl.when(pl.program_id(0) == 0)
     def _():
         run(low)
 
-    @pl.when(pl.program_id(0) >= half)
+    @pl.when(pl.program_id(0) == 1)
     def _():
         run(high)
 
 
 def back(low, high, weight, features, before, first, rows):
-    blocks, size, width = features.shape
-    steps = 4
-    group = blocks // steps
-    half = steps // 2
-    specs = [pl.BlockSpec((group, rows, width), lambda i: (jnp.minimum(i, half - 1), 0, 0))] * 4
-    specs += [pl.BlockSpec((group, rows, width), lambda i: (jnp.maximum(i - half, 0), 0, 0))] * 4
-    specs += [
-        pl.BlockSpec(weight.shape, lambda i: (0, 0)),
-        pl.BlockSpec((group, size, width), lambda i: (i, 0, 0)),
-    ]
+    blocks, strips, strip, width = features.shape
+    half, steps, skip = blocks // 2, rows // strip, first // strip
+    piece = pl.BlockSpec((half, 1, strip, width), lambda i, j: (i, skip + j, 0, 0))
+    specs = [
+        pl.BlockSpec((half, strip, width), lambda i, j: (0, jnp.where(i == 0, j, steps - 1), 0))
+    ] * 4
+    specs += [pl.BlockSpec((half, strip, width), lambda i, j: (0, jnp.where(i == 0, 0, j), 0))] * 4
+    specs += [pl.BlockSpec(weight.shape, lambda i, j: (0, 0)), piece]
     args = [*low, *high, weight, features]
-    if first:
-        specs.append(pl.BlockSpec((group, first, width), lambda i: (i, 0, 0)))
+    aliases = {}
+    if before is not None:
+        specs.append(pl.BlockSpec(memory_space=pl.ANY))
         args.append(before)
+        aliases = {len(args) - 1: 0}
     return pl.pallas_call(
-        functools.partial(back_kernel, half=half, first=first, rows=rows),
-        grid=(steps,),
+        back_kernel,
+        grid=(2, steps),
         in_specs=specs,
-        out_specs=pl.BlockSpec((group, first + rows, width), lambda i: (i, 0, 0)),
-        out_shape=jax.ShapeDtypeStruct((blocks, first + rows, width), jnp.bfloat16),
+        out_specs=piece,
+        out_shape=jax.ShapeDtypeStruct(features.shape, jnp.bfloat16),
+        input_output_aliases=aliases,
         compiler_params=pltpu.CompilerParams(vmem_limit_bytes=VMEM_BACK),
         cost_estimate=pl.CostEstimate(
             flops=2 * blocks * rows * width * weight.shape[0],
@@ -258,8 +271,8 @@
     scaled = (grad_out.astype(jnp.float32) * scale[:, None]).astype(jnp.bfloat16)
     owner = tile_owner[:, 0]
     weight_mine = weight_rows(weight)
-    blocked = features.reshape(blocks, size, width)
-    wide_scale = jnp.broadcast_to(scale.reshape(blocks, size, 1), (blocks, size, width))
+    blocked = features.reshape(blocks, size // STRIP, STRIP, width)
+    block_scale = scale.reshape(blocks, size)
 
     starts = [sum(SPLIT[:k]) for k in range(len(SPLIT))]
     gathered = lax.all_gather(features, "col", axis=0).reshape(cols, blocks, size, width)
@@ -274,7 +287,7 @@
 
     tags = incoming[0][:, PLACES * SPLIT[0], :PLACES].astype(jnp.int32).reshape(-1)
     tags = jnp.where(tags < 0, blocks, tags)
-    scales = [wide_scale[:, first : first + rows] for first, rows in zip(starts, SPLIT)]
+    scales = [block_scale[:, first : first + rows] for first, rows in zip(starts, SPLIT)]
 
     def local_terms(own, first, rows):
         return lax.dot_general(
@@ -298,7 +311,8 @@
     terms = terms + local_terms(own, *SPLIT)
     norm_factor = 1.0 / math.sqrt(node_rows * peers)
     share = cols * width // peers
-    total = jnp.sum(exchange(terms.reshape(peers, share, width)), axis=0) * norm_factor
+    pieces = exchange(terms.reshape(peers, share, width).astype(jnp.bfloat16))
+    total = jnp.sum(pieces.astype(jnp.float32), axis=0) * norm_factor
     total = jnp.broadcast_to(total.astype(jnp.bfloat16)[None], (peers, share, width))
     near, _ = lax.optimization_barrier((near, total))
     far = col_far(near[0], near[3])

time: 296 us -> 295 us (level)
  Pallas kernels: 34.1 us -> 40.5 us
  local copies, waits for them, and re-layouts: 5.91 us -> 1.33 us
  matrix products: 8.02 us -> 4.49 us
    all_to_all x4, waiting for transfers between devices: 85.8 us -> 80.6 us  [exchange(): return lax.all_to_all(block, 'row', split_axis=0, concat_axis=0, tiled=True)]
    pallas_call x2, Pallas kernels: 6.9 us -> 11.4 us  [back(): pl.pallas_call(back_kernel, grid=(2, steps), in_specs=specs, out_specs=pi...]
    dot_general x2, matrix products: 8.02 us -> 4.49 us  [local_terms(): lax.dot_general(gathered[:, :, first:first + rows], jnp.concatenate(own,...]
  transfers between devices with their start and end apart: 20 -> 20, of which waited for: 10 -> 12; matrix products, arithmetic and copies ran while one was open for 5% -> 3% of each run, Pallas kernels for 9% -> 11%
where the time goes in v3:
time: 295 us; the launch traced here: 292 us
  waiting for transfers between devices  174 us (59%)
  starting transfers between devices  49 us (17%)
  Pallas kernels  40.5 us (14%)
  between operations  14.9 us (5%)
  other arithmetic  7.46 us (3%)
  matrix products  4.49 us (2%)
    all_to_all x4, waiting for transfers between devices, exchange(): return lax.all_to_all(block, 'row', split_axis=0, concat_axis=0, tiled=True)  80.6 us
    all_gather x1, waiting for transfers between devices, per_device(): lax.all_gather(features, 'col', axis=0).reshape(cols, blocks, size, width)  50.7 us
    all_to_all x4, starting transfers between devices, exchange(): return lax.all_to_all(block, 'row', split_axis=0, concat_axis=0, tiled=True)  31.3 us
    pallas_call x2, Pallas kernels, products(): pl.pallas_call(functools.partial(product_kernel, first=first, rows=rows,...  20.5 us
    ppermute x2, waiting for transfers between devices, col_far(): lax.ppermute(low_left, 'col', ring(1, size))  15.1 us
    ppermute x2, waiting for transfers between devices, col_near(): low_left = lax.ppermute(low, 'col', ahead)  12.9 us
    pallas_call x2, Pallas kernels, back(): pl.pallas_call(back_kernel, grid=(2, steps), in_specs=specs, out_specs=pi...  11.4 us
    ppermute x2, waiting for transfers between devices, col_near(): low_right = lax.ppermute(low, 'col', behind)  11 us
  transfers between devices with their start and end apart: 20, of which 12 were waited for; matrix products, arithmetic and copies ran while one was open for 3% of the time, Pallas kernels for 11%

profile of v3, /device:TPU:1, one launch (start us, length us, event | category | flops | bytes accessed | tf_op | source)
XLA Modules:
  0.0 292.0 jit_solution(12821267426081130794)
XLA Ops:
  9.3 2.2 multiply_convert_fusion.scaled
  11.6 9.5 %products.2 = bf16[64,328,128]{2,1,0:T(8,128)(2,1)} custom-call(s32[192]{0:T(256)} %row_block.3, s32[192]{0:T(256)} %bitcast.31, s32[192]{0:T(256)} %local.3, s32[1]{0:T(128)S(6)} %copy.34.live, bf16[192,128,128]{2,1,0:T(8,128)(2,1)} %tiles.3, bf16[8192,128]{1,0:T(8,128)(2,1)} %multiply_convert_fusion.scaled), custom_call_target="tpu_custom_call" | custom-call | flops 503316480 | bytes 13631488 | tf_op jit(solution)/shard_map/products/pallas_call | solution.py:75
  21.1 13.5 %all-to-all-start = ((bf16[64,328,128]{2,1,0:T(8,128)(2,1)}), bf16[64,328,128]{2,1,0:T(8,128)(2,1)}, u32[]{:S(2)}, u32[]{:S(2)}) async-start(bf16[64,328,128]{2,1,0:T(8,128)(2,1)} %products.2), calls=%async_computation | async-start | bytes 10747904 | tf_op jit(solution)/shard_map/all_to_all | solution.py:224
  34.8 2.6 collective-permute-start.2
  38.9 11.0 %products.3 = bf16[64,192,128]{2,1,0:T(8,128)(2,1)} custom-call(s32[192]{0:T(256)} %row_block.3, s32[192]{0:T(256)} %bitcast.32, s32[192]{0:T(256)} %local.3, s32[1]{0:T(128)S(6)} %copy.34.live, bf16[192,128,128]{2,1,0:T(8,128)(2,1)} %tiles.3, bf16[8192,128]{1,0:T(8,128)(2,1)} %multiply_convert_fusion.scaled), custom_call_target="tpu_custom_call" | custom-call | flops 301989888 | bytes 11534336 | tf_op jit(solution)/shard_map/products/pallas_call | solution.py:75
  50.0 50.7 %all-gather.3.cloned.1.call-done = bf16[32768,128]{1,0:T(8,128)(2,1)} async-done(((bf16[8192,128]{1,0:T(8,128)(2,1)}), bf16[32768,128]{1,0:T(8,128)(2,1)}) %all-gather.3.cloned.1.call-update) | async-done | bytes 8388624 | tf_op jit(solution)/shard_map/all_gather | solution.py:278
  100.7 55.1 %all-to-all-done.incoming = bf16[64,328,128]{2,1,0:T(8,128)(2,1)} async-done(((bf16[64,328,128]{2,1,0:T(8,128)(2,1)}), bf16[64,328,128]{2,1,0:T(8,128)(2,1)}, u32[]{:S(2)}, u32[]{:S(2)}) %all-to-all-start) | async-done | bytes 5373984 | tf_op jit(solution)/shard_map/all_to_all | solution.py:224
  155.8 6.0 %all-to-all-start.1 = ((bf16[64,192,128]{2,1,0:T(8,128)(2,1)}), bf16[64,192,128]{2,1,0:T(8,128)(2,1)}, u32[]{:S(2)}, u32[]{:S(2)}) async-start(bf16[64,192,128]{2,1,0:T(8,128)(2,1)} %products.3), calls=%async_computation.1 | async-start | bytes 6291456 | tf_op jit(solution)/shard_map/all_to_all | solution.py:224
  163.0 4.7 %sums.2 = (bf16[32,80,128]{2,1,0:T(8,128)(2,1)S(1)}, bf16[32,80,128]{2,1,0:T(8,128)(2,1)S(1)}) custom-call(s32[256]{0:T(256)S(1)} %compare_select_fusion.labels, bf16[64,328,128]{2,1,0:T(8,128)(2,1)} %all-to-all-done.incoming, f32[64,80]{1,0:T(8,128)S(1)} %bitcast.29), custom_call_target="tpu_custom_call" | custom-call | flops 2686976 | bytes 6684672 | tf_op jit(solution)/shard_map/sums/pallas_call | solution.py:141
  171.9 12.9 %collective-permute-done.3.refs_1_ = bf16[32,80,128]{2,1,0:T(8,128)(2,1)S(1)} collective-permute-done((bf16[32,80,128]{2,1,0:T(8,128)(2,1)S(1)}, bf16[32,80,128]{2,1,0:T(8,128)(2,1)S(1)}, u32[]{:S(2)}, u32[]{:S(2)}) %collective-permute-start.3) | collective-permute-done | bytes 655392 | tf_op jit(solution)/shard_map/ppermute | solution.py:229
  184.8 2.7 collective-permute-start.8
  187.5 11.0 %collective-permute-done.5.refs_3_ = bf16[32,80,128]{2,1,0:T(8,128)(2,1)S(1)} collective-permute-done((bf16[32,80,128]{2,1,0:T(8,128)(2,1)S(1)}, bf16[32,80,128]{2,1,0:T(8,128)(2,1)S(1)}, u32[]{:S(2)}, u32[]{:S(2)}) %collective-permute-start.5) | collective-permute-done | bytes 655392 | tf_op jit(solution)/shard_map/ppermute | solution.py:232
  198.8 14.0 %collective-permute-done.4.refs_2_ = bf16[32,80,128]{2,1,0:T(8,128)(2,1)S(1)} collective-permute-done((bf16[32,80,128]{2,1,0:T(8,128)(2,1)S(1)}, bf16[32,80,128]{2,1,0:T(8,128)(2,1)S(1)}, u32[]{:S(2)}, u32[]{:S(2)}) %collective-permute-start.4) | collective-permute-done | bytes 655392 | tf_op jit(solution)/shard_map/ppermute | solution.py:239
  212.9 5.8 %back.2.refs_10_ = bf16[64,8,16,128]{3,2,1,0:T(8,128)(2,1)} custom-call(bf16[32,80,128]{2,1,0:T(8,128)(2,1)S(1)} %get-tuple-element.19.refs_0_, bf16[32,80,128]{2,1,0:T(8,128)(2,1)S(1)} %collective-permute-done.3.refs_1_, bf16[32,80,128]{2,1,0:T(8,128)(2,1)S(1)} %collective-permute-done.4.refs_2_, bf16[32,80,128]{2,1,0:T(8,128)(2,1)S(1)} %collective-permute-done.5.refs_3_, ...), custom_call_target="tpu_custom_call" | custom-call | flops 671088640 | bytes 7864320 | tf_op jit(solution)/shard_map/back/pallas_call | solution.py:202
  220.2 14.9 %all-to-all-done.1.incoming = bf16[64,192,128]{2,1,0:T(8,128)(2,1)} async-done(((bf16[64,192,128]{2,1,0:T(8,128)(2,1)}), bf16[64,192,128]{2,1,0:T(8,128)(2,1)}, u32[]{:S(2)}, u32[]{:S(2)}) %all-to-all-start.1) | async-done | bytes 3145760 | tf_op jit(solution)/shard_map/all_to_all | solution.py:224
  235.2 4.0 %sums.3 = (bf16[32,48,128]{2,1,0:T(8,128)(2,1)S(1)}, bf16[32,48,128]{2,1,0:T(8,128)(2,1)S(1)}) custom-call(s32[256]{0:T(256)S(1)} %compare_select_fusion.labels, bf16[64,192,128]{2,1,0:T(8,128)(2,1)} %all-to-all-done.1.incoming, f32[64,48]{1,0:T(8,128)S(1)} %slice.21.scale), custom_call_target="tpu_custom_call" | custom-call | flops 1572864 | bytes 3932160 | tf_op jit(solution)/shard_map/sums/pallas_call | solution.py:141
  239.2 2.9 %fusion.9 = f32[4,128,128]{2,1,0:T(8,128)S(1)} fusion(bf16[4,64,128,128]{3,2,1,0:T(8,128)(2,1)} %bitcast.33, bf16[32,48,128]{2,1,0:T(8,128)(2,1)S(1)} %get-tuple-element.25.refs_4_, bf16[32,48,128]{2,1,0:T(8,128)(2,1)S(1)} %get-tuple-element.24.refs_0_), kind=kOutput, calls=%fused_computation.9 | convolution fusion | flops 403046400 | bytes 4194304 | tf_op jit(solution)/shard_map/dot_general | solution.py:293
  242.8 6.3 %all-to-all-start.2 = ((bf16[64,8,128]{2,1,0:T(8,128)(2,1)}), bf16[64,8,128]{2,1,0:T(8,128)(2,1)}, u32[]{:S(2)}, u32[]{:S(2)}) async-start(bf16[64,8,128]{2,1,0:T(8,128)(2,1)} %bitcast.11), calls=%async_computation.2 | async-start | bytes 262144 | tf_op jit(solution)/shard_map/all_to_all | solution.py:224
  253.3 6.1 %all-to-all-done.2 = bf16[64,8,128]{2,1,0:T(8,128)(2,1)} async-done(((bf16[64,8,128]{2,1,0:T(8,128)(2,1)}), bf16[64,8,128]{2,1,0:T(8,128)(2,1)}, u32[]{:S(2)}, u32[]{:S(2)}) %all-to-all-start.2) | async-done | bytes 131104 | tf_op jit(solution)/shard_map/all_to_all | solution.py:224
  261.0 5.6 %all-to-all-start.3 = ((bf16[64,8,128]{2,1,0:T(8,128)(2,1)}), bf16[64,8,128]{2,1,0:T(8,128)(2,1)}, u32[]{:S(2)}, u32[]{:S(2)}) async-start(bf16[64,8,128]{2,1,0:T(8,128)(2,1)} %broadcast_in_dim.12), calls=%async_computation.3 | async-start | bytes 262144 | tf_op jit(solution)/shard_map/all_to_all | solution.py:224
  266.6 2.4 collective-permute-done.10.refs_5_
  270.6 1.8 collective-permute-start.14
  272.3 4.6 %all-to-all-done.3 = bf16[64,8,128]{2,1,0:T(8,128)(2,1)} async-done(((bf16[64,8,128]{2,1,0:T(8,128)(2,1)}), bf16[64,8,128]{2,1,0:T(8,128)(2,1)}, u32[]{:S(2)}, u32[]{:S(2)}) %all-to-all-start.3) | async-done | bytes 131104 | tf_op jit(solution)/shard_map/all_to_all | solution.py:224
  279.6 5.6 %back.3 = bf16[64,8,16,128]{3,2,1,0:T(8,128)(2,1)} custom-call(bf16[32,48,128]{2,1,0:T(8,128)(2,1)S(1)} %get-tuple-element.24.refs_0_, bf16[32,48,128]{2,1,0:T(8,128)(2,1)S(1)} %collective-permute-done.9.refs_1_, bf16[32,48,128]{2,1,0:T(8,128)(2,1)} %collective-permute-done.13.refs_2_, ...), custom_call_target="tpu_custom_call", output_to_operand_aliasing={{}: (10, {})} | custom-call | flops 402653184 | bytes 4718592 | tf_op jit(solution)/shard_map/back/pallas_call | solution.py:202
  (50 shorter events, 21.5 us)
Async XLA Ops:
  7.2 2.2 copy-start.1
  7.2 93.5 %all-gather.3.cloned.1.call-start = ((), (), s32[]{:S(2)}) async-start(), calls=%async_computation.4 | async-start | bytes 10485760 | tf_op jit(solution)/shard_map/all_gather | solution.py:278
  21.1 13.5 %copy-start.2 = (bf16[512,128]{1,0:T(8,128)(2,1)S(1)}, bf16[512,128]{1,0:T(8,128)(2,1)}, u32[]{:S(2)}) copy-start(bf16[512,128]{1,0:T(8,128)(2,1)} %param.11) | copy-start | bytes 393220
  21.1 134.7 %all-to-all-start = ((bf16[64,328,128]{2,1,0:T(8,128)(2,1)}), bf16[64,328,128]{2,1,0:T(8,128)(2,1)}, u32[]{:S(2)}, u32[]{:S(2)}) async-start(bf16[64,328,128]{2,1,0:T(8,128)(2,1)} %products.2), calls=%async_computation | async-start | bytes 10747904 | tf_op jit(solution)/shard_map/all_to_all | solution.py:224
  34.8 15.2 %collective-permute-start.2 = (bf16[128,128]{0,1:T(8,128)(2,1)S(1)}, bf16[128,128]{0,1:T(8,128)(2,1)S(1)}, u32[]{:S(2)}, u32[]{:S(2)}) collective-permute-start(bf16[128,128]{0,1:T(8,128)(2,1)S(1)} %copy.32), channel_id=1, source_target_pairs={{0,3},{1,0},{2,1},{3,2},{4,7},{5,4},{6,5},{7,6},{8,11},{9,8},{10,9... | collective-permute-start | bytes 98312 | tf_op jit(solution)/shard_map/ppermute | solution.py:258
  37.4 12.5 %collective-permute-start.1 = (bf16[128,128]{0,1:T(8,128)(2,1)S(1)}, bf16[128,128]{0,1:T(8,128)(2,1)S(1)}, u32[]{:S(2)}, u32[]{:S(2)}) collective-permute-start(bf16[128,128]{0,1:T(8,128)(2,1)S(1)} %copy.31), channel_id=1, source_target_pairs={{0,2},{1,3},{2,0},{3,1},{4,6},{5,7},{6,4},{7,5},{8,10},{9,11},{10,... | collective-permute-start | bytes 98312 | tf_op jit(solution)/shard_map/ppermute | solution.py:258
  38.2 11.8 %collective-permute-start = (bf16[128,128]{0,1:T(8,128)(2,1)S(1)}, bf16[128,128]{0,1:T(8,128)(2,1)S(1)}, u32[]{:S(2)}, u32[]{:S(2)}) collective-permute-start(bf16[128,128]{0,1:T(8,128)(2,1)S(1)} %copy.30), channel_id=1, source_target_pairs={{0,1},{1,2},{2,3},{3,0},{4,5},{5,6},{6,7},{7,4},{8,9},{9,10},{10,1... | collective-permute-start | bytes 98312 | tf_op jit(solution)/shard_map/ppermute | solution.py:258
  155.8 79.4 %all-to-all-start.1 = ((bf16[64,192,128]{2,1,0:T(8,128)(2,1)}), bf16[64,192,128]{2,1,0:T(8,128)(2,1)}, u32[]{:S(2)}, u32[]{:S(2)}) async-start(bf16[64,192,128]{2,1,0:T(8,128)(2,1)} %products.3), calls=%async_computation.1 | async-start | bytes 6291456 | tf_op jit(solution)/shard_map/all_to_all | solution.py:224
  161.7 51.2 %copy-start = (bf16[8192,128]{1,0:T(8,128)(2,1)S(1)}, bf16[8192,128]{1,0:T(8,128)(2,1)}, u32[]{:S(2)}) copy-start(bf16[8192,128]{1,0:T(8,128)(2,1)} %param.10) | copy-start | bytes 6291460
  167.7 17.1 %collective-permute-start.3 = (bf16[32,80,128]{2,1,0:T(8,128)(2,1)S(1)}, bf16[32,80,128]{2,1,0:T(8,128)(2,1)S(1)}, u32[]{:S(2)}, u32[]{:S(2)}) collective-permute-start(bf16[32,80,128]{2,1,0:T(8,128)(2,1)S(1)} %get-tuple-element.19.refs_0_), channel_id=1, source_target_pairs={{0,1},{1,2},{2,3},{3,0},{4,5},{5,6},{6,7},{7,4},{8,9},{9,10},{10,1... | collective-permute-start | bytes 1966088 | tf_op jit(solution)/shard_map/ppermute | solution.py:229
  169.0 15.8 %collective-permute-start.7 = (bf16[32,80,128]{2,1,0:T(8,128)(2,1)S(1)}, bf16[32,80,128]{2,1,0:T(8,128)(2,1)S(1)}, u32[]{:S(2)}, u32[]{:S(2)}) collective-permute-start(bf16[32,80,128]{2,1,0:T(8,128)(2,1)S(1)} %get-tuple-element.20.refs_4_), channel_id=1, source_target_pairs={{0,3},{1,0},{2,1},{3,2},{4,7},{5,4},{6,5},{7,6},{8,11},{9,8},{10,9... | collective-permute-start | bytes 1966088 | tf_op jit(solution)/shard_map/ppermute | solution.py:230
  170.4 28.1 %collective-permute-start.5 = (bf16[32,80,128]{2,1,0:T(8,128)(2,1)S(1)}, bf16[32,80,128]{2,1,0:T(8,128)(2,1)S(1)}, u32[]{:S(2)}, u32[]{:S(2)}) collective-permute-start(bf16[32,80,128]{2,1,0:T(8,128)(2,1)S(1)} %get-tuple-element.19.refs_0_), channel_id=1, source_target_pairs={{0,3},{1,0},{2,1},{3,2},{4,7},{5,4},{6,5},{7,6},{8,11},{9,8},{10,9... | collective-permute-start | bytes 1966088 | tf_op jit(solution)/shard_map/ppermute | solution.py:232
  171.7 27.1 %collective-permute-start.6 = (bf16[32,80,128]{2,1,0:T(8,128)(2,1)S(1)}, bf16[32,80,128]{2,1,0:T(8,128)(2,1)S(1)}, u32[]{:S(2)}, u32[]{:S(2)}) collective-permute-start(bf16[32,80,128]{2,1,0:T(8,128)(2,1)S(1)} %get-tuple-element.20.refs_4_), channel_id=1, source_target_pairs={{0,1},{1,2},{2,3},{3,0},{4,5},{5,6},{6,7},{7,4},{8,9},{9,10},{10,1... | collective-permute-start | bytes 1966088 | tf_op jit(solution)/shard_map/ppermute | solution.py:231
  184.8 28.1 %collective-permute-start.4 = (bf16[32,80,128]{2,1,0:T(8,128)(2,1)S(1)}, bf16[32,80,128]{2,1,0:T(8,128)(2,1)S(1)}, u32[]{:S(2)}, u32[]{:S(2)}) collective-permute-start(bf16[32,80,128]{2,1,0:T(8,128)(2,1)S(1)} %collective-permute-done.3.refs_1_), channel_id=1, source_target_pairs={{0,1},{1,2},{2,3},{3,0},{4,5},{5,6},{6,7},{7,4},{8,9},{9,10},{10,1... | collective-permute-start | bytes 1966088 | tf_op jit(solution)/shard_map/ppermute | solution.py:239
  184.8 28.1 %collective-permute-start.8 = (bf16[32,80,128]{2,1,0:T(8,128)(2,1)S(1)}, bf16[32,80,128]{2,1,0:T(8,128)(2,1)S(1)}, u32[]{:S(2)}, u32[]{:S(2)}) collective-permute-start(bf16[32,80,128]{2,1,0:T(8,128)(2,1)S(1)} %collective-permute-done.7.refs_7_), channel_id=1, source_target_pairs={{0,3},{1,0},{2,1},{3,2},{4,7},{5,4},{6,5},{7,6},{8,11},{9,8},{10,9... | collective-permute-start | bytes 1966088 | tf_op jit(solution)/shard_map/ppermute | solution.py:240
  212.9 5.8 %copy-start.3 = (bf16[32768,128]{1,0:T(8,128)(2,1)S(1)}, bf16[32768,128]{1,0:T(8,128)(2,1)}, u32[]{:S(2)}) copy-start(bf16[32768,128]{1,0:T(8,128)(2,1)} %all-gather.3.cloned.1.call-done) | copy-start | bytes 25165828
  242.8 16.6 %all-to-all-start.2 = ((bf16[64,8,128]{2,1,0:T(8,128)(2,1)}), bf16[64,8,128]{2,1,0:T(8,128)(2,1)}, u32[]{:S(2)}, u32[]{:S(2)}) async-start(bf16[64,8,128]{2,1,0:T(8,128)(2,1)} %bitcast.11), calls=%async_computation.2 | async-start | bytes 262144 | tf_op jit(solution)/shard_map/all_to_all | solution.py:224
  249.1 17.5 %collective-permute-start.9 = (bf16[32,48,128]{2,1,0:T(8,128)(2,1)S(1)}, bf16[32,48,128]{2,1,0:T(8,128)(2,1)S(1)}, u32[]{:S(2)}, u32[]{:S(2)}) collective-permute-start(bf16[32,48,128]{2,1,0:T(8,128)(2,1)S(1)} %get-tuple-element.24.refs_0_), channel_id=1, source_target_pairs={{0,1},{1,2},{2,3},{3,0},{4,5},{5,6},{6,7},{7,4},{8,9},{9,10},{10,1... | collective-permute-start | bytes 1179656 | tf_op jit(solution)/shard_map/ppermute | solution.py:229
  250.4 18.7 %collective-permute-start.10 = (bf16[32,48,128]{2,1,0:T(8,128)(2,1)S(1)}, bf16[32,48,128]{2,1,0:T(8,128)(2,1)}, u32[]{:S(2)}, u32[]{:S(2)}) collective-permute-start(bf16[32,48,128]{2,1,0:T(8,128)(2,1)S(1)} %get-tuple-element.25.refs_4_), channel_id=1, source_target_pairs={{0,1},{1,2},{2,3},{3,0},{4,5},{5,6},{6,7},{7,4},{8,9},{9,10},{10,1... | collective-permute-start | bytes 1179656 | tf_op jit(solution)/shard_map/ppermute | solution.py:231
  251.6 17.5 %collective-permute-start.11 = (bf16[32,48,128]{2,1,0:T(8,128)(2,1)S(1)}, bf16[32,48,128]{2,1,0:T(8,128)(2,1)}, u32[]{:S(2)}, u32[]{:S(2)}) collective-permute-start(bf16[32,48,128]{2,1,0:T(8,128)(2,1)S(1)} %get-tuple-element.24.refs_0_), channel_id=1, source_target_pairs={{0,3},{1,0},{2,1},{3,2},{4,7},{5,4},{6,5},{7,6},{8,11},{9,8},{10,9... | collective-permute-start | bytes 1179656 | tf_op jit(solution)/shard_map/ppermute | solution.py:232
  253.1 16.6 %collective-permute-start.12 = (bf16[32,48,128]{2,1,0:T(8,128)(2,1)S(1)}, bf16[32,48,128]{2,1,0:T(8,128)(2,1)}, u32[]{:S(2)}, u32[]{:S(2)}) collective-permute-start(bf16[32,48,128]{2,1,0:T(8,128)(2,1)S(1)} %get-tuple-element.25.refs_4_), channel_id=1, source_target_pairs={{0,3},{1,0},{2,1},{3,2},{4,7},{5,4},{6,5},{7,6},{8,11},{9,8},{10,9... | collective-permute-start | bytes 1179656 | tf_op jit(solution)/shard_map/ppermute | solution.py:230
  261.0 15.9 %all-to-all-start.3 = ((bf16[64,8,128]{2,1,0:T(8,128)(2,1)}), bf16[64,8,128]{2,1,0:T(8,128)(2,1)}, u32[]{:S(2)}, u32[]{:S(2)}) async-start(bf16[64,8,128]{2,1,0:T(8,128)(2,1)} %broadcast_in_dim.12), calls=%async_computation.3 | async-start | bytes 262144 | tf_op jit(solution)/shard_map/all_to_all | solution.py:224
  269.7 9.9 %collective-permute-start.13 = (bf16[32,48,128]{2,1,0:T(8,128)(2,1)S(1)}, bf16[32,48,128]{2,1,0:T(8,128)(2,1)}, u32[]{:S(2)}, u32[]{:S(2)}) collective-permute-start(bf16[32,48,128]{2,1,0:T(8,128)(2,1)S(1)} %collective-permute-done.9.refs_1_), channel_id=1, source_target_pairs={{0,1},{1,2},{2,3},{3,0},{4,5},{5,6},{6,7},{7,4},{8,9},{9,10},{10,1... | collective-permute-start | bytes 1179656 | tf_op jit(solution)/shard_map/ppermute | solution.py:239
  270.6 9.0 %collective-permute-start.14 = (bf16[32,48,128]{2,1,0:T(8,128)(2,1)}, bf16[32,48,128]{2,1,0:T(8,128)(2,1)}, u32[]{:S(2)}, u32[]{:S(2)}) collective-permute-start(bf16[32,48,128]{2,1,0:T(8,128)(2,1)} %collective-permute-done.12.refs_7_), channel_id=1, source_target_pairs={{0,3},{1,0},{2,1},{3,2},{4,7},{5,4},{6,5},{7,6},{8,11},{9,8},{10,9... | collective-permute-start | bytes 1179656 | tf_op jit(solution)/shard_map/ppermute | solution.py:240
Sparse Core Ops, SparseCore 0:
  9.8 90.8 all-gather.2

commit v4 on v3

--- a/solution.py
+++ b/solution.py
@@ -11,6 +11,7 @@
 PLACES = 4
 LABEL_ROWS = 8
 STRIP = 16
+BACK_STEPS = 4
 SPLIT = (80, 48)
 VMEM_PRODUCTS = 54 * 1024 * 1024
 VMEM_SUMS = 48 * 1024 * 1024
@@ -163,36 +164,39 @@
     )(labels, incoming, scale)
 
 
-def back_kernel(*refs):
+def back_kernel(*refs, half):
     low, high, (weight, features), out = refs[:4], refs[4:8], refs[8:10], refs[-1]
-    half, _, strip, width = features.shape
+    group, strips, strip, width = features.shape
+    nodes = group * strips * strip
 
     def run(parts):
-        whole = jnp.concatenate([part[...].reshape(half * strip, width) for part in parts], axis=1)
+        whole = jnp.concatenate([part[...].reshape(nodes, width) for part in parts], axis=1)
         back = lax.dot_general(
             whole, weight[...], (((1,), (0,)), ((), ())), preferred_element_type=jnp.float32
         ).reshape(features.shape)
         mask = features[...].astype(jnp.float32) > 0
         out[...] = jnp.where(mask, back, 0.0).astype(out.dtype)
 
-    @pl.when(pl.program_id(0) == 0)
+    @pl.when(pl.program_id(0) < half)
     def _():
         run(low)
 
-    @pl.when(pl.program_id(0) == 1)
+    @pl.when(pl.program_id(0) >= half)
     def _():
         run(high)
 
 
 def back(low, high, weight, features, before, first, rows):
     blocks, strips, strip, width = features.shape
-    half, steps, skip = blocks // 2, rows // strip, first // strip
-    piece = pl.BlockSpec((half, 1, strip, width), lambda i, j: (i, skip + j, 0, 0))
-    specs = [
-        pl.BlockSpec((half, strip, width), lambda i, j: (0, jnp.where(i == 0, j, steps - 1), 0))
-    ] * 4
-    specs += [pl.BlockSpec((half, strip, width), lambda i, j: (0, jnp.where(i == 0, 0, j), 0))] * 4
-    specs += [pl.BlockSpec(weight.shape, lambda i, j: (0, 0)), piece]
+    steps = BACK_STEPS
+    group, half, skip = blocks // steps, steps // 2, first // strip
+    piece = pl.BlockSpec(
+        (pl.Element(group), pl.Element(rows // strip), pl.Element(strip), pl.Element(width)),
+        lambda i: (i * group, skip, 0, 0),
+    )
+    specs = [pl.BlockSpec((group, rows, width), lambda i: (jnp.minimum(i, half - 1), 0, 0))] * 4
+    specs += [pl.BlockSpec((group, rows, width), lambda i: (jnp.maximum(i - half, 0), 0, 0))] * 4
+    specs += [pl.BlockSpec(weight.shape, lambda i: (0, 0)), piece]
     args = [*low, *high, weight, features]
     aliases = {}
     if before is not None:
@@ -200,8 +204,8 @@
         args.append(before)
         aliases = {len(args) - 1: 0}
     return pl.pallas_call(
-        back_kernel,
-        grid=(2, steps),
+        functools.partial(back_kernel, half=half),
+        grid=(steps,),
         in_specs=specs,
         out_specs=piece,
         out_shape=jax.ShapeDtypeStruct(features.shape, jnp.bfloat16),

time: 295 us -> 294 us (level)
  Pallas kernels: 40.5 us -> 36.8 us
    pallas_call x2, Pallas kernels: 11.4 us -> 7.62 us  [back(): pl.pallas_call(functools.partial(back_kernel, half=half), grid=(steps,),...]
  transfers between devices with their start and end apart: 20 -> 20, of which waited for: 12 -> 12; matrix products, arithmetic and copies ran while one was open for 3% -> 3% of each run, Pallas kernels for 11% -> 10%
where the time goes in v4:
time: 294 us; the launch traced here: 291 us
  waiting for transfers between devices  176 us (60%)
  starting transfers between devices  49 us (17%)
  Pallas kernels  36.8 us (13%)
  between operations  14.9 us (5%)
  other arithmetic  7.46 us (3%)
  matrix products  4.49 us (2%)
    all_to_all x4, waiting for transfers between devices, exchange(): return lax.all_to_all(block, 'row', split_axis=0, concat_axis=0, tiled=True)  82.5 us
    all_gather x1, waiting for transfers between devices, per_device(): lax.all_gather(features, 'col', axis=0).reshape(cols, blocks, size, width)  50.8 us
    all_to_all x4, starting transfers between devices, exchange(): return lax.all_to_all(block, 'row', split_axis=0, concat_axis=0, tiled=True)  31.3 us
    pallas_call x2, Pallas kernels, products(): pl.pallas_call(functools.partial(product_kernel, first=first, rows=rows,...  20.5 us
    ppermute x2, waiting for transfers between devices, col_far(): lax.ppermute(low_left, 'col', ring(1, size))  15.1 us
    ppermute x2, waiting for transfers between devices, col_near(): low_left = lax.ppermute(low, 'col', ahead)  12.9 us
    ppermute x2, waiting for transfers between devices, col_near(): low_right = lax.ppermute(low, 'col', behind)  11 us
    pallas_call x2, Pallas kernels, sums(): pl.pallas_call(functools.partial(sum_kernel, rows=rows), in_specs=[pl.Blo...  8.64 us
  transfers between devices with their start and end apart: 20, of which 12 were waited for; matrix products, arithmetic and copies ran while one was open for 3% of the time, Pallas kernels for 10%

profile of v4, /device:TPU:1, one launch (start us, length us, event | category | flops | bytes accessed | tf_op | source)
XLA Modules:
  0.0 290.9 jit_solution(5396949294328091063)
XLA Ops:
  9.3 2.2 multiply_convert_fusion.scaled
  11.6 9.5 %products.2 = bf16[64,328,128]{2,1,0:T(8,128)(2,1)} custom-call(s32[192]{0:T(256)} %row_block.3, s32[192]{0:T(256)} %bitcast.31, s32[192]{0:T(256)} %local.3, s32[1]{0:T(128)S(6)} %copy.34.live, bf16[192,128,128]{2,1,0:T(8,128)(2,1)} %tiles.3, bf16[8192,128]{1,0:T(8,128)(2,1)} %multiply_convert_fusion.scaled), custom_call_target="tpu_custom_call" | custom-call | flops 503316480 | bytes 13631488 | tf_op jit(solution)/shard_map/products/pallas_call | solution.py:76
  21.1 13.5 %all-to-all-start = ((bf16[64,328,128]{2,1,0:T(8,128)(2,1)}), bf16[64,328,128]{2,1,0:T(8,128)(2,1)}, u32[]{:S(2)}, u32[]{:S(2)}) async-start(bf16[64,328,128]{2,1,0:T(8,128)(2,1)} %products.2), calls=%async_computation | async-start | bytes 10747904 | tf_op jit(solution)/shard_map/all_to_all | solution.py:228
  34.8 2.6 collective-permute-start.2
  38.9 11.0 %products.3 = bf16[64,192,128]{2,1,0:T(8,128)(2,1)} custom-call(s32[192]{0:T(256)} %row_block.3, s32[192]{0:T(256)} %bitcast.32, s32[192]{0:T(256)} %local.3, s32[1]{0:T(128)S(6)} %copy.34.live, bf16[192,128,128]{2,1,0:T(8,128)(2,1)} %tiles.3, bf16[8192,128]{1,0:T(8,128)(2,1)} %multiply_convert_fusion.scaled), custom_call_target="tpu_custom_call" | custom-call | flops 301989888 | bytes 11534336 | tf_op jit(solution)/shard_map/products/pallas_call | solution.py:76
  50.0 50.8 %all-gather.3.cloned.1.call-done = bf16[32768,128]{1,0:T(8,128)(2,1)} async-done(((bf16[8192,128]{1,0:T(8,128)(2,1)}), bf16[32768,128]{1,0:T(8,128)(2,1)}) %all-gather.3.cloned.1.call-update) | async-done | bytes 8388624 | tf_op jit(solution)/shard_map/all_gather | solution.py:282
  100.7 55.0 %all-to-all-done.incoming = bf16[64,328,128]{2,1,0:T(8,128)(2,1)} async-done(((bf16[64,328,128]{2,1,0:T(8,128)(2,1)}), bf16[64,328,128]{2,1,0:T(8,128)(2,1)}, u32[]{:S(2)}, u32[]{:S(2)}) %all-to-all-start) | async-done | bytes 5373984 | tf_op jit(solution)/shard_map/all_to_all | solution.py:228
  155.8 6.0 %all-to-all-start.1 = ((bf16[64,192,128]{2,1,0:T(8,128)(2,1)}), bf16[64,192,128]{2,1,0:T(8,128)(2,1)}, u32[]{:S(2)}, u32[]{:S(2)}) async-start(bf16[64,192,128]{2,1,0:T(8,128)(2,1)} %products.3), calls=%async_computation.1 | async-start | bytes 6291456 | tf_op jit(solution)/shard_map/all_to_all | solution.py:228
  163.0 4.7 %sums.2 = (bf16[32,80,128]{2,1,0:T(8,128)(2,1)S(1)}, bf16[32,80,128]{2,1,0:T(8,128)(2,1)S(1)}) custom-call(s32[256]{0:T(256)S(1)} %compare_select_fusion.labels, bf16[64,328,128]{2,1,0:T(8,128)(2,1)} %all-to-all-done.incoming, f32[64,80]{1,0:T(8,128)S(1)} %bitcast.29), custom_call_target="tpu_custom_call" | custom-call | flops 2686976 | bytes 6684672 | tf_op jit(solution)/shard_map/sums/pallas_call | solution.py:142
  171.9 12.9 %collective-permute-done.3.refs_1_ = bf16[32,80,128]{2,1,0:T(8,128)(2,1)S(1)} collective-permute-done((bf16[32,80,128]{2,1,0:T(8,128)(2,1)S(1)}, bf16[32,80,128]{2,1,0:T(8,128)(2,1)S(1)}, u32[]{:S(2)}, u32[]{:S(2)}) %collective-permute-start.3) | collective-permute-done | bytes 655392 | tf_op jit(solution)/shard_map/ppermute | solution.py:233
  184.8 2.7 collective-permute-start.8
  187.6 11.0 %collective-permute-done.5.refs_3_ = bf16[32,80,128]{2,1,0:T(8,128)(2,1)S(1)} collective-permute-done((bf16[32,80,128]{2,1,0:T(8,128)(2,1)S(1)}, bf16[32,80,128]{2,1,0:T(8,128)(2,1)S(1)}, u32[]{:S(2)}, u32[]{:S(2)}) %collective-permute-start.5) | collective-permute-done | bytes 655392 | tf_op jit(solution)/shard_map/ppermute | solution.py:236
  198.9 14.0 %collective-permute-done.4.refs_2_ = bf16[32,80,128]{2,1,0:T(8,128)(2,1)S(1)} collective-permute-done((bf16[32,80,128]{2,1,0:T(8,128)(2,1)S(1)}, bf16[32,80,128]{2,1,0:T(8,128)(2,1)S(1)}, u32[]{:S(2)}, u32[]{:S(2)}) %collective-permute-start.4) | collective-permute-done | bytes 655392 | tf_op jit(solution)/shard_map/ppermute | solution.py:243
  212.9 3.1 %back.2.refs_10_ = bf16[64,8,16,128]{3,2,1,0:T(8,128)(2,1)} custom-call(bf16[32,80,128]{2,1,0:T(8,128)(2,1)S(1)} %get-tuple-element.19.refs_0_, bf16[32,80,128]{2,1,0:T(8,128)(2,1)S(1)} %collective-permute-done.3.refs_1_, bf16[32,80,128]{2,1,0:T(8,128)(2,1)S(1)} %collective-permute-done.4.refs_2_, bf16[32,80,128]{2,1,0:T(8,128)(2,1)S(1)} %collective-permute-done.5.refs_3_, ...), custom_call_target="tpu_custom_call" | custom-call | flops 671088640 | bytes 7864320 | tf_op jit(solution)/shard_map/back/pallas_call | solution.py:206
  218.3 16.8 %all-to-all-done.1.incoming = bf16[64,192,128]{2,1,0:T(8,128)(2,1)} async-done(((bf16[64,192,128]{2,1,0:T(8,128)(2,1)}), bf16[64,192,128]{2,1,0:T(8,128)(2,1)}, u32[]{:S(2)}, u32[]{:S(2)}) %all-to-all-start.1) | async-done | bytes 3145760 | tf_op jit(solution)/shard_map/all_to_all | solution.py:228
  235.2 4.0 %sums.3 = (bf16[32,48,128]{2,1,0:T(8,128)(2,1)S(1)}, bf16[32,48,128]{2,1,0:T(8,128)(2,1)S(1)}) custom-call(s32[256]{0:T(256)S(1)} %compare_select_fusion.labels, bf16[64,192,128]{2,1,0:T(8,128)(2,1)} %all-to-all-done.1.incoming, f32[64,48]{1,0:T(8,128)S(1)} %slice.21.scale), custom_call_target="tpu_custom_call" | custom-call | flops 1572864 | bytes 3932160 | tf_op jit(solution)/shard_map/sums/pallas_call | solution.py:142
  239.1 2.9 %fusion.9 = f32[4,128,128]{2,1,0:T(8,128)S(1)} fusion(bf16[4,64,128,128]{3,2,1,0:T(8,128)(2,1)} %bitcast.33, bf16[32,48,128]{2,1,0:T(8,128)(2,1)S(1)} %get-tuple-element.25.refs_4_, bf16[32,48,128]{2,1,0:T(8,128)(2,1)S(1)} %get-tuple-element.24.refs_0_), kind=kOutput, calls=%fused_computation.9 | convolution fusion | flops 403046400 | bytes 4194304 | tf_op jit(solution)/shard_map/dot_general | solution.py:297
  242.8 6.3 %all-to-all-start.2 = ((bf16[64,8,128]{2,1,0:T(8,128)(2,1)}), bf16[64,8,128]{2,1,0:T(8,128)(2,1)}, u32[]{:S(2)}, u32[]{:S(2)}) async-start(bf16[64,8,128]{2,1,0:T(8,128)(2,1)} %bitcast.11), calls=%async_computation.2 | async-start | bytes 262144 | tf_op jit(solution)/shard_map/all_to_all | solution.py:228
  253.3 6.1 %all-to-all-done.2 = bf16[64,8,128]{2,1,0:T(8,128)(2,1)} async-done(((bf16[64,8,128]{2,1,0:T(8,128)(2,1)}), bf16[64,8,128]{2,1,0:T(8,128)(2,1)}, u32[]{:S(2)}, u32[]{:S(2)}) %all-to-all-start.2) | async-done | bytes 131104 | tf_op jit(solution)/shard_map/all_to_all | solution.py:228
  261.0 5.6 %all-to-all-start.3 = ((bf16[64,8,128]{2,1,0:T(8,128)(2,1)}), bf16[64,8,128]{2,1,0:T(8,128)(2,1)}, u32[]{:S(2)}, u32[]{:S(2)}) async-start(bf16[64,8,128]{2,1,0:T(8,128)(2,1)} %broadcast_in_dim.12), calls=%async_computation.3 | async-start | bytes 262144 | tf_op jit(solution)/shard_map/all_to_all | solution.py:228
  266.6 2.4 collective-permute-done.10.refs_5_
  270.5 1.8 collective-permute-start.14
  272.3 4.6 %all-to-all-done.3 = bf16[64,8,128]{2,1,0:T(8,128)(2,1)} async-done(((bf16[64,8,128]{2,1,0:T(8,128)(2,1)}), bf16[64,8,128]{2,1,0:T(8,128)(2,1)}, u32[]{:S(2)}, u32[]{:S(2)}) %all-to-all-start.3) | async-done | bytes 131104 | tf_op jit(solution)/shard_map/all_to_all | solution.py:228
  279.5 4.5 %back.3 = bf16[64,8,16,128]{3,2,1,0:T(8,128)(2,1)} custom-call(bf16[32,48,128]{2,1,0:T(8,128)(2,1)S(1)} %get-tuple-element.24.refs_0_, bf16[32,48,128]{2,1,0:T(8,128)(2,1)S(1)} %collective-permute-done.9.refs_1_, bf16[32,48,128]{2,1,0:T(8,128)(2,1)} %collective-permute-done.13.refs_2_, ...), custom_call_target="tpu_custom_call", output_to_operand_aliasing={{}: (10, {})} | custom-call | flops 402653184 | bytes 4718592 | tf_op jit(solution)/shard_map/back/pallas_call | solution.py:206
  (50 shorter events, 22.2 us)
Async XLA Ops:
  7.2 2.2 copy-start.1
  7.2 93.5 %all-gather.3.cloned.1.call-start = ((), (), s32[]{:S(2)}) async-start(), calls=%async_computation.4 | async-start | bytes 10485760 | tf_op jit(solution)/shard_map/all_gather | solution.py:282
  21.1 13.5 %copy-start.2 = (bf16[512,128]{1,0:T(8,128)(2,1)S(1)}, bf16[512,128]{1,0:T(8,128)(2,1)}, u32[]{:S(2)}) copy-start(bf16[512,128]{1,0:T(8,128)(2,1)} %param.11) | copy-start | bytes 393220
  21.1 134.7 %all-to-all-start = ((bf16[64,328,128]{2,1,0:T(8,128)(2,1)}), bf16[64,328,128]{2,1,0:T(8,128)(2,1)}, u32[]{:S(2)}, u32[]{:S(2)}) async-start(bf16[64,328,128]{2,1,0:T(8,128)(2,1)} %products.2), calls=%async_computation | async-start | bytes 10747904 | tf_op jit(solution)/shard_map/all_to_all | solution.py:228
  34.8 15.2 %collective-permute-start.2 = (bf16[128,128]{0,1:T(8,128)(2,1)S(1)}, bf16[128,128]{0,1:T(8,128)(2,1)S(1)}, u32[]{:S(2)}, u32[]{:S(2)}) collective-permute-start(bf16[128,128]{0,1:T(8,128)(2,1)S(1)} %copy.32), channel_id=1, source_target_pairs={{0,3},{1,0},{2,1},{3,2},{4,7},{5,4},{6,5},{7,6},{8,11},{9,8},{10,9... | collective-permute-start | bytes 98312 | tf_op jit(solution)/shard_map/ppermute | solution.py:262
  37.4 12.5 %collective-permute-start.1 = (bf16[128,128]{0,1:T(8,128)(2,1)S(1)}, bf16[128,128]{0,1:T(8,128)(2,1)S(1)}, u32[]{:S(2)}, u32[]{:S(2)}) collective-permute-start(bf16[128,128]{0,1:T(8,128)(2,1)S(1)} %copy.31), channel_id=1, source_target_pairs={{0,2},{1,3},{2,0},{3,1},{4,6},{5,7},{6,4},{7,5},{8,10},{9,11},{10,... | collective-permute-start | bytes 98312 | tf_op jit(solution)/shard_map/ppermute | solution.py:262
  38.1 11.8 %collective-permute-start = (bf16[128,128]{0,1:T(8,128)(2,1)S(1)}, bf16[128,128]{0,1:T(8,128)(2,1)S(1)}, u32[]{:S(2)}, u32[]{:S(2)}) collective-permute-start(bf16[128,128]{0,1:T(8,128)(2,1)S(1)} %copy.30), channel_id=1, source_target_pairs={{0,1},{1,2},{2,3},{3,0},{4,5},{5,6},{6,7},{7,4},{8,9},{9,10},{10,1... | collective-permute-start | bytes 98312 | tf_op jit(solution)/shard_map/ppermute | solution.py:262
  155.8 79.4 %all-to-all-start.1 = ((bf16[64,192,128]{2,1,0:T(8,128)(2,1)}), bf16[64,192,128]{2,1,0:T(8,128)(2,1)}, u32[]{:S(2)}, u32[]{:S(2)}) async-start(bf16[64,192,128]{2,1,0:T(8,128)(2,1)} %products.3), calls=%async_computation.1 | async-start | bytes 6291456 | tf_op jit(solution)/shard_map/all_to_all | solution.py:228
  161.7 51.2 %copy-start = (bf16[8192,128]{1,0:T(8,128)(2,1)S(1)}, bf16[8192,128]{1,0:T(8,128)(2,1)}, u32[]{:S(2)}) copy-start(bf16[8192,128]{1,0:T(8,128)(2,1)} %param.10) | copy-start | bytes 6291460
  167.7 17.2 %collective-permute-start.3 = (bf16[32,80,128]{2,1,0:T(8,128)(2,1)S(1)}, bf16[32,80,128]{2,1,0:T(8,128)(2,1)S(1)}, u32[]{:S(2)}, u32[]{:S(2)}) collective-permute-start(bf16[32,80,128]{2,1,0:T(8,128)(2,1)S(1)} %get-tuple-element.19.refs_0_), channel_id=1, source_target_pairs={{0,1},{1,2},{2,3},{3,0},{4,5},{5,6},{6,7},{7,4},{8,9},{9,10},{10,1... | collective-permute-start | bytes 1966088 | tf_op jit(solution)/shard_map/ppermute | solution.py:233
  169.0 15.9 %collective-permute-start.7 = (bf16[32,80,128]{2,1,0:T(8,128)(2,1)S(1)}, bf16[32,80,128]{2,1,0:T(8,128)(2,1)S(1)}, u32[]{:S(2)}, u32[]{:S(2)}) collective-permute-start(bf16[32,80,128]{2,1,0:T(8,128)(2,1)S(1)} %get-tuple-element.20.refs_4_), channel_id=1, source_target_pairs={{0,3},{1,0},{2,1},{3,2},{4,7},{5,4},{6,5},{7,6},{8,11},{9,8},{10,9... | collective-permute-start | bytes 1966088 | tf_op jit(solution)/shard_map/ppermute | solution.py:234
  170.4 28.1 %collective-permute-start.5 = (bf16[32,80,128]{2,1,0:T(8,128)(2,1)S(1)}, bf16[32,80,128]{2,1,0:T(8,128)(2,1)S(1)}, u32[]{:S(2)}, u32[]{:S(2)}) collective-permute-start(bf16[32,80,128]{2,1,0:T(8,128)(2,1)S(1)} %get-tuple-element.19.refs_0_), channel_id=1, source_target_pairs={{0,3},{1,0},{2,1},{3,2},{4,7},{5,4},{6,5},{7,6},{8,11},{9,8},{10,9... | collective-permute-start | bytes 1966088 | tf_op jit(solution)/shard_map/ppermute | solution.py:236
  171.7 27.2 %collective-permute-start.6 = (bf16[32,80,128]{2,1,0:T(8,128)(2,1)S(1)}, bf16[32,80,128]{2,1,0:T(8,128)(2,1)S(1)}, u32[]{:S(2)}, u32[]{:S(2)}) collective-permute-start(bf16[32,80,128]{2,1,0:T(8,128)(2,1)S(1)} %get-tuple-element.20.refs_4_), channel_id=1, source_target_pairs={{0,1},{1,2},{2,3},{3,0},{4,5},{5,6},{6,7},{7,4},{8,9},{9,10},{10,1... | collective-permute-start | bytes 1966088 | tf_op jit(solution)/shard_map/ppermute | solution.py:235
  184.8 28.1 %collective-permute-start.4 = (bf16[32,80,128]{2,1,0:T(8,128)(2,1)S(1)}, bf16[32,80,128]{2,1,0:T(8,128)(2,1)S(1)}, u32[]{:S(2)}, u32[]{:S(2)}) collective-permute-start(bf16[32,80,128]{2,1,0:T(8,128)(2,1)S(1)} %collective-permute-done.3.refs_1_), channel_id=1, source_target_pairs={{0,1},{1,2},{2,3},{3,0},{4,5},{5,6},{6,7},{7,4},{8,9},{9,10},{10,1... | collective-permute-start | bytes 1966088 | tf_op jit(solution)/shard_map/ppermute | solution.py:243
  184.8 28.1 %collective-permute-start.8 = (bf16[32,80,128]{2,1,0:T(8,128)(2,1)S(1)}, bf16[32,80,128]{2,1,0:T(8,128)(2,1)S(1)}, u32[]{:S(2)}, u32[]{:S(2)}) collective-permute-start(bf16[32,80,128]{2,1,0:T(8,128)(2,1)S(1)} %collective-permute-done.7.refs_7_), channel_id=1, source_target_pairs={{0,3},{1,0},{2,1},{3,2},{4,7},{5,4},{6,5},{7,6},{8,11},{9,8},{10,9... | collective-permute-start | bytes 1966088 | tf_op jit(solution)/shard_map/ppermute | solution.py:244
  212.9 3.9 %copy-start.3 = (bf16[32768,128]{1,0:T(8,128)(2,1)S(1)}, bf16[32768,128]{1,0:T(8,128)(2,1)}, u32[]{:S(2)}) copy-start(bf16[32768,128]{1,0:T(8,128)(2,1)} %all-gather.3.cloned.1.call-done) | copy-start | bytes 25165828
  242.8 16.6 %all-to-all-start.2 = ((bf16[64,8,128]{2,1,0:T(8,128)(2,1)}), bf16[64,8,128]{2,1,0:T(8,128)(2,1)}, u32[]{:S(2)}, u32[]{:S(2)}) async-start(bf16[64,8,128]{2,1,0:T(8,128)(2,1)} %bitcast.11), calls=%async_computation.2 | async-start | bytes 262144 | tf_op jit(solution)/shard_map/all_to_all | solution.py:228
  249.1 17.5 %collective-permute-start.9 = (bf16[32,48,128]{2,1,0:T(8,128)(2,1)S(1)}, bf16[32,48,128]{2,1,0:T(8,128)(2,1)S(1)}, u32[]{:S(2)}, u32[]{:S(2)}) collective-permute-start(bf16[32,48,128]{2,1,0:T(8,128)(2,1)S(1)} %get-tuple-element.24.refs_0_), channel_id=1, source_target_pairs={{0,1},{1,2},{2,3},{3,0},{4,5},{5,6},{6,7},{7,4},{8,9},{9,10},{10,1... | collective-permute-start | bytes 1179656 | tf_op jit(solution)/shard_map/ppermute | solution.py:233
  250.4 18.7 %collective-permute-start.10 = (bf16[32,48,128]{2,1,0:T(8,128)(2,1)S(1)}, bf16[32,48,128]{2,1,0:T(8,128)(2,1)}, u32[]{:S(2)}, u32[]{:S(2)}) collective-permute-start(bf16[32,48,128]{2,1,0:T(8,128)(2,1)S(1)} %get-tuple-element.25.refs_4_), channel_id=1, source_target_pairs={{0,1},{1,2},{2,3},{3,0},{4,5},{5,6},{6,7},{7,4},{8,9},{9,10},{10,1... | collective-permute-start | bytes 1179656 | tf_op jit(solution)/shard_map/ppermute | solution.py:235
  251.6 17.5 %collective-permute-start.11 = (bf16[32,48,128]{2,1,0:T(8,128)(2,1)S(1)}, bf16[32,48,128]{2,1,0:T(8,128)(2,1)}, u32[]{:S(2)}, u32[]{:S(2)}) collective-permute-start(bf16[32,48,128]{2,1,0:T(8,128)(2,1)S(1)} %get-tuple-element.24.refs_0_), channel_id=1, source_target_pairs={{0,3},{1,0},{2,1},{3,2},{4,7},{5,4},{6,5},{7,6},{8,11},{9,8},{10,9... | collective-permute-start | bytes 1179656 | tf_op jit(solution)/shard_map/ppermute | solution.py:236
  253.0 16.6 %collective-permute-start.12 = (bf16[32,48,128]{2,1,0:T(8,128)(2,1)S(1)}, bf16[32,48,128]{2,1,0:T(8,128)(2,1)}, u32[]{:S(2)}, u32[]{:S(2)}) collective-permute-start(bf16[32,48,128]{2,1,0:T(8,128)(2,1)S(1)} %get-tuple-element.25.refs_4_), channel_id=1, source_target_pairs={{0,3},{1,0},{2,1},{3,2},{4,7},{5,4},{6,5},{7,6},{8,11},{9,8},{10,9... | collective-permute-start | bytes 1179656 | tf_op jit(solution)/shard_map/ppermute | solution.py:234
  261.0 15.9 %all-to-all-start.3 = ((bf16[64,8,128]{2,1,0:T(8,128)(2,1)}), bf16[64,8,128]{2,1,0:T(8,128)(2,1)}, u32[]{:S(2)}, u32[]{:S(2)}) async-start(bf16[64,8,128]{2,1,0:T(8,128)(2,1)} %broadcast_in_dim.12), calls=%async_computation.3 | async-start | bytes 262144 | tf_op jit(solution)/shard_map/all_to_all | solution.py:228
  269.6 9.9 %collective-permute-start.13 = (bf16[32,48,128]{2,1,0:T(8,128)(2,1)S(1)}, bf16[32,48,128]{2,1,0:T(8,128)(2,1)}, u32[]{:S(2)}, u32[]{:S(2)}) collective-permute-start(bf16[32,48,128]{2,1,0:T(8,128)(2,1)S(1)} %collective-permute-done.9.refs_1_), channel_id=1, source_target_pairs={{0,1},{1,2},{2,3},{3,0},{4,5},{5,6},{6,7},{7,4},{8,9},{9,10},{10,1... | collective-permute-start | bytes 1179656 | tf_op jit(solution)/shard_map/ppermute | solution.py:243
  270.5 9.0 %collective-permute-start.14 = (bf16[32,48,128]{2,1,0:T(8,128)(2,1)}, bf16[32,48,128]{2,1,0:T(8,128)(2,1)}, u32[]{:S(2)}, u32[]{:S(2)}) collective-permute-start(bf16[32,48,128]{2,1,0:T(8,128)(2,1)} %collective-permute-done.12.refs_7_), channel_id=1, source_target_pairs={{0,3},{1,0},{2,1},{3,2},{4,7},{5,4},{6,5},{7,6},{8,11},{9,8},{10,9... | collective-permute-start | bytes 1179656 | tf_op jit(solution)/shard_map/ppermute | solution.py:244
Sparse Core Ops, SparseCore 0:
  9.8 90.8 all-gather.2

commit v5 on v4

--- a/solution.py
+++ b/solution.py
@@ -12,7 +12,7 @@
 LABEL_ROWS = 8
 STRIP = 16
 BACK_STEPS = 4
-SPLIT = (80, 48)
+SPLIT = (96, 32)
 VMEM_PRODUCTS = 54 * 1024 * 1024
 VMEM_SUMS = 48 * 1024 * 1024
 VMEM_BACK = 16 * 1024 * 1024
@@ -306,13 +306,12 @@
     far = col_far(near[0], near[3])
     terms = local_terms(own, 0, SPLIT[0])
     before = back(*pair_up(own, near, far), weight_mine, blocked, None, 0, SPLIT[0])
-    incoming[1], scales[1], terms, before = lax.optimization_barrier(
-        (incoming[1], scales[1], terms, before)
-    )
+    incoming[1], terms, _ = lax.optimization_barrier((incoming[1], terms, near))
 
     own = sums(tags, incoming[1], scales[1], SPLIT[1])
     near = col_near(*own)
     terms = terms + local_terms(own, *SPLIT)
+    terms, _ = lax.optimization_barrier((terms, far))
     norm_factor = 1.0 / math.sqrt(node_rows * peers)
     share = cols * width // peers
     pieces = exchange(terms.reshape(peers, share, width).astype(jnp.bfloat16))

time: 294 us -> 298 us (1.014)
  waiting for transfers between devices: 176 us -> 164 us
  starting transfers between devices: 49 us -> 55.2 us
  local copies, waits for them, and re-layouts: 2.08 us -> 8.05 us
  matrix products: 4.49 us -> 7.87 us
    all_gather x1, waiting for transfers between devices: 50.8 us -> 72.7 us  [per_device(): lax.all_gather(features, 'col', axis=0).reshape(cols, blocks, size, width)]
    all_to_all x4, waiting for transfers between devices: 82.5 us -> 66.7 us  [exchange(): return lax.all_to_all(block, 'row', split_axis=0, concat_axis=0, tiled=True)]
    ppermute x2, waiting for transfers between devices: 15.1 us -> 0.99 us  [col_far(): lax.ppermute(low_left, 'col', ring(1, size))]
    ppermute x2, waiting for transfers between devices: 11 us -> 0.01 us  [col_near(): low_right = lax.ppermute(low, 'col', behind)]
    ppermute x2, waiting for transfers between devices: 2.76 us -> 8.72 us  [col_near(): high_left = lax.ppermute(high, 'col', ahead)]
    unnamed x12 -> x24, local copies, waits for them, and re-layouts: 1.21 us -> 6.58 us
    all_to_all x4, starting transfers between devices: 31.3 us -> 36.2 us  [exchange(): return lax.all_to_all(block, 'row', split_axis=0, concat_axis=0, tiled=True)]
    dot_general x2, matrix products: 4.49 us -> 7.87 us  [local_terms(): lax.dot_general(gathered[:, :, first:first + rows], jnp.concatenate(own,...]
  transfers between devices with their start and end apart: 20 -> 20, of which waited for: 12 -> 7; matrix products, arithmetic and copies ran while one was open for 3% -> 5% of each run, Pallas kernels for 10% -> 9%
where the time goes in v5:
time: 298 us; the launch traced here: 297 us
  waiting for transfers between devices  164 us (55%)
  starting transfers between devices  55.2 us (19%)
  Pallas kernels  38.9 us (13%)
  between operations  14.9 us (5%)
  other arithmetic  8.53 us (3%)
  local copies, waits for them, and re-layouts  8.05 us (3%)
  matrix products  7.87 us (3%)
    all_gather x1, waiting for transfers between devices, per_device(): lax.all_gather(features, 'col', axis=0).reshape(cols, blocks, size, width)  72.7 us
    all_to_all x4, waiting for transfers between devices, exchange(): return lax.all_to_all(block, 'row', split_axis=0, concat_axis=0, tiled=True)  66.7 us
    all_to_all x4, starting transfers between devices, exchange(): return lax.all_to_all(block, 'row', split_axis=0, concat_axis=0, tiled=True)  36.2 us
    pallas_call x2, Pallas kernels, products(): pl.pallas_call(functools.partial(product_kernel, first=first, rows=rows,...  20.7 us
    ppermute x2, waiting for transfers between devices, col_near(): low_left = lax.ppermute(low, 'col', ahead)  13.9 us
    pallas_call x2, Pallas kernels, back(): pl.pallas_call(functools.partial(back_kernel, half=half), grid=(steps,),...  9.41 us
    pallas_call x2, Pallas kernels, sums(): pl.pallas_call(functools.partial(sum_kernel, rows=rows), in_specs=[pl.Blo...  8.88 us
    ppermute x2, waiting for transfers between devices, col_near(): high_left = lax.ppermute(high, 'col', ahead)  8.72 us
  transfers between devices with their start and end apart: 20, of which 7 were waited for; matrix products, arithmetic and copies ran while one was open for 5% of the time, Pallas kernels for 9%

profile of v5, /device:TPU:1, one launch (start us, length us, event | category | flops | bytes accessed | tf_op | source)
XLA Modules:
  0.0 297.3 jit_solution(15009309724250633998)
XLA Ops:
  8.6 3.4 %multiply_convert_fusion.scaled = bf16[8192,128]{1,0:T(8,128)(2,1)} fusion(bf16[8192,128]{1,0:T(8,128)(2,1)} %param.9, f32[8192]{0:T(1024)S(1)} %get-tuple-element.35), kind=kLoop, calls=%fused_computation.2 | loop fusion | flops 3145728 | bytes 4227072 | tf_op jit(solution)/shard_map/convert_element_type | solution.py:275
  12.0 9.3 %products.2 = bf16[64,392,128]{2,1,0:T(8,128)(2,1)} custom-call(s32[192]{0:T(256)} %row_block.3, s32[192]{0:T(256)} %bitcast.32, s32[192]{0:T(256)} %local.3, s32[1]{0:T(128)S(6)} %copy.34.live, bf16[192,128,128]{2,1,0:T(8,128)(2,1)} %tiles.3, bf16[8192,128]{1,0:T(8,128)(2,1)} %multiply_convert_fusion.scaled), custom_call_target="tpu_custom_call" | custom-call | flops 603979776 | bytes 14680064 | tf_op jit(solution)/shard_map/products/pallas_call | solution.py:76
  21.4 13.3 %all-to-all-start = ((bf16[64,392,128]{2,1,0:T(8,128)(2,1)}), bf16[64,392,128]{2,1,0:T(8,128)(2,1)}, u32[]{:S(2)}, u32[]{:S(2)}) async-start(bf16[64,392,128]{2,1,0:T(8,128)(2,1)} %products.2), calls=%async_computation | async-start | bytes 12845056 | tf_op jit(solution)/shard_map/all_to_all | solution.py:228
  35.7 2.6 collective-permute-start.2
  39.9 11.3 %products.3 = bf16[64,128,128]{2,1,0:T(8,128)(2,1)} custom-call(s32[192]{0:T(256)} %row_block.3, s32[192]{0:T(256)} %bitcast.33, s32[192]{0:T(256)} %local.3, s32[1]{0:T(128)S(6)} %copy.34.live, bf16[192,128,128]{2,1,0:T(8,128)(2,1)} %tiles.3, bf16[8192,128]{1,0:T(8,128)(2,1)} %multiply_convert_fusion.scaled), custom_call_target="tpu_custom_call" | custom-call | flops 201326592 | bytes 10485760 | tf_op jit(solution)/shard_map/products/pallas_call | solution.py:76
  51.3 72.7 %all-gather.3.cloned.1.call-done = bf16[32768,128]{1,0:T(8,128)(2,1)} async-done(((bf16[8192,128]{1,0:T(8,128)(2,1)}), bf16[32768,128]{1,0:T(8,128)(2,1)}) %all-gather.3.cloned.1.call-update) | async-done | bytes 8388624 | tf_op jit(solution)/shard_map/all_gather | solution.py:282
  124.0 54.3 %all-to-all-done.incoming = bf16[64,392,128]{2,1,0:T(8,128)(2,1)} async-done(((bf16[64,392,128]{2,1,0:T(8,128)(2,1)}), bf16[64,392,128]{2,1,0:T(8,128)(2,1)}, u32[]{:S(2)}, u32[]{:S(2)}) %all-to-all-start) | async-done | bytes 6422560 | tf_op jit(solution)/shard_map/all_to_all | solution.py:228
  178.4 5.8 %all-to-all-start.1 = ((bf16[64,128,128]{2,1,0:T(8,128)(2,1)}), bf16[64,128,128]{2,1,0:T(8,128)(2,1)S(1)}, u32[]{:S(2)}, u32[]{:S(2)}) async-start(bf16[64,128,128]{2,1,0:T(8,128)(2,1)} %products.3), calls=%async_computation.1 | async-start | bytes 4194304 | tf_op jit(solution)/shard_map/all_to_all | solution.py:228
  185.3 5.1 %sums.2 = (bf16[32,96,128]{2,1,0:T(8,128)(2,1)S(1)}, bf16[32,96,128]{2,1,0:T(8,128)(2,1)S(1)}) custom-call(s32[256]{0:T(256)S(1)} %compare_select_fusion.labels, bf16[64,392,128]{2,1,0:T(8,128)(2,1)} %all-to-all-done.incoming, f32[64,96]{1,0:T(8,128)S(1)} %bitcast.29), custom_call_target="tpu_custom_call" | custom-call | flops 3211264 | bytes 7995392 | tf_op jit(solution)/shard_map/sums/pallas_call | solution.py:142
  193.2 2.7 collective-permute-start.5
  196.5 13.9 %collective-permute-done.3.refs_1_ = bf16[32,96,128]{2,1,0:T(8,128)(2,1)} collective-permute-done((bf16[32,96,128]{2,1,0:T(8,128)(2,1)S(1)}, bf16[32,96,128]{2,1,0:T(8,128)(2,1)}, u32[]{:S(2)}, u32[]{:S(2)}) %collective-permute-start.3) | collective-permute-done | bytes 786464 | tf_op jit(solution)/shard_map/ppermute | solution.py:233
  210.5 2.7 collective-permute-start.12
  213.1 5.3 %fusion.9 = f32[4,128,128]{2,1,0:T(8,128)} fusion(bf16[32,96,128]{2,1,0:T(8,128)(2,1)S(1)} %get-tuple-element.19.refs_4_, bf16[32,96,128]{2,1,0:T(8,128)(2,1)S(1)} %get-tuple-element.18.refs_0_, bf16[4,64,128,128]{3,2,1,0:T(8,128)(2,1)} %bitcast.34), kind=kOutput, calls=%fused_computation.9 | convolution fusion | flops 806092800 | bytes 8126464 | tf_op jit(solution)/shard_map/dot_general | solution.py:297
  218.5 8.7 %collective-permute-done.4.refs_5_ = bf16[32,96,128]{2,1,0:T(8,128)(2,1)S(1)} collective-permute-done((bf16[32,96,128]{2,1,0:T(8,128)(2,1)S(1)}, bf16[32,96,128]{2,1,0:T(8,128)(2,1)S(1)}, u32[]{:S(2)}, u32[]{:S(2)}) %collective-permute-start.4) | collective-permute-done | bytes 786464 | tf_op jit(solution)/shard_map/ppermute | solution.py:235
  229.0 6.4 %all-to-all-done.1.incoming = bf16[64,128,128]{2,1,0:T(8,128)(2,1)S(1)} async-done(((bf16[64,128,128]{2,1,0:T(8,128)(2,1)}), bf16[64,128,128]{2,1,0:T(8,128)(2,1)S(1)}, u32[]{:S(2)}, u32[]{:S(2)}) %all-to-all-start.1) | async-done | bytes 2097184 | tf_op jit(solution)/shard_map/all_to_all | solution.py:228
  236.2 3.8 %sums.3 = (bf16[32,32,128]{2,1,0:T(8,128)(2,1)S(1)}, bf16[32,32,128]{2,1,0:T(8,128)(2,1)S(1)}) custom-call(s32[256]{0:T(256)S(1)} %compare_select_fusion.labels, bf16[64,128,128]{2,1,0:T(8,128)(2,1)S(1)} %all-to-all-done.1.incoming, f32[64,32]{1,0:T(8,128)S(1)} %copy-done.7), custom_call_target="tpu_custom_call" | custom-call | flops 1048576 | bytes 2621440 | tf_op jit(solution)/shard_map/sums/pallas_call | solution.py:142
  239.9 2.5 fusion.6
  244.2 11.5 %all-to-all-start.2 = ((bf16[64,8,128]{2,1,0:T(8,128)(2,1)}), bf16[64,8,128]{2,1,0:T(8,128)(2,1)}, u32[]{:S(2)}, u32[]{:S(2)}) async-start(bf16[64,8,128]{2,1,0:T(8,128)(2,1)} %bitcast.31), calls=%async_computation.2 | async-start | bytes 262144 | tf_op jit(solution)/shard_map/all_to_all | solution.py:228
  257.9 1.8 collective-permute-start.9
  260.0 6.0 %all-to-all-done.2 = bf16[64,8,128]{2,1,0:T(8,128)(2,1)} async-done(((bf16[64,8,128]{2,1,0:T(8,128)(2,1)}), bf16[64,8,128]{2,1,0:T(8,128)(2,1)}, u32[]{:S(2)}, u32[]{:S(2)}) %all-to-all-start.2) | async-done | bytes 131104 | tf_op jit(solution)/shard_map/all_to_all | solution.py:228
  267.6 5.6 %all-to-all-start.3 = ((bf16[64,8,128]{2,1,0:T(8,128)(2,1)}), bf16[64,8,128]{2,1,0:T(8,128)(2,1)}, u32[]{:S(2)}, u32[]{:S(2)}) async-start(bf16[64,8,128]{2,1,0:T(8,128)(2,1)} %broadcast_in_dim.12), calls=%async_computation.3 | async-start | bytes 262144 | tf_op jit(solution)/shard_map/all_to_all | solution.py:228
  279.4 5.2 %back.2.refs_10_ = bf16[64,8,16,128]{3,2,1,0:T(8,128)(2,1)} custom-call(bf16[32,96,128]{2,1,0:T(8,128)(2,1)S(1)} %get-tuple-element.18.refs_0_, bf16[32,96,128]{2,1,0:T(8,128)(2,1)} %collective-permute-done.3.refs_1_, bf16[32,96,128]{2,1,0:T(8,128)(2,1)} %collective-permute-done.11.refs_2_, bf16[32,96,128]{2,1,0:T(8,128)(2,1)S(1)} %copy-done.6, ...), custom_call_target="tpu_custom_call" | custom-call | flops 805306368 | bytes 9437184 | tf_op jit(solution)/shard_map/back/pallas_call | solution.py:206
  284.6 1.6 bitcast_convert_fusion
  286.3 4.2 %back.3 = bf16[64,8,16,128]{3,2,1,0:T(8,128)(2,1)} custom-call(bf16[32,32,128]{2,1,0:T(8,128)(2,1)S(1)} %get-tuple-element.21.refs_0_, bf16[32,32,128]{2,1,0:T(8,128)(2,1)} %collective-permute-done.7.refs_1_, bf16[32,32,128]{2,1,0:T(8,128)(2,1)} %collective-permute-done.13.refs_2_, ...), custom_call_target="tpu_custom_call", output_to_operand_aliasing={{}: (10, {})} | custom-call | flops 268435456 | bytes 3145728 | tf_op jit(solution)/shard_map/back/pallas_call | solution.py:206
  (62 shorter events, 22.6 us)
Async XLA Ops:
  21.4 157.0 %all-to-all-start = ((bf16[64,392,128]{2,1,0:T(8,128)(2,1)}), bf16[64,392,128]{2,1,0:T(8,128)(2,1)}, u32[]{:S(2)}, u32[]{:S(2)}) async-start(bf16[64,392,128]{2,1,0:T(8,128)(2,1)} %products.2), calls=%async_computation | async-start | bytes 12845056 | tf_op jit(solution)/shard_map/all_to_all | solution.py:228
  34.7 89.3 %all-gather.3.cloned.1.call-start = ((), (), s32[]{:S(2)}) async-start(), calls=%async_computation.4 | async-start | bytes 10485760 | tf_op jit(solution)/shard_map/all_gather | solution.py:282
  35.7 15.5 %collective-permute-start.2 = (bf16[128,128]{0,1:T(8,128)(2,1)S(1)}, bf16[128,128]{0,1:T(8,128)(2,1)S(1)}, u32[]{:S(2)}, u32[]{:S(2)}) collective-permute-start(bf16[128,128]{0,1:T(8,128)(2,1)S(1)} %copy.32), channel_id=1, source_target_pairs={{0,3},{1,0},{2,1},{3,2},{4,7},{5,4},{6,5},{7,6},{8,11},{9,8},{10,9... | collective-permute-start | bytes 98312 | tf_op jit(solution)/shard_map/ppermute | solution.py:262
  38.4 12.9 %collective-permute-start.1 = (bf16[128,128]{0,1:T(8,128)(2,1)S(1)}, bf16[128,128]{0,1:T(8,128)(2,1)S(1)}, u32[]{:S(2)}, u32[]{:S(2)}) collective-permute-start(bf16[128,128]{0,1:T(8,128)(2,1)S(1)} %copy.31), channel_id=1, source_target_pairs={{0,2},{1,3},{2,0},{3,1},{4,6},{5,7},{6,4},{7,5},{8,10},{9,11},{10,... | collective-permute-start | bytes 98312 | tf_op jit(solution)/shard_map/ppermute | solution.py:262
  39.1 12.1 %collective-permute-start = (bf16[128,128]{0,1:T(8,128)(2,1)S(1)}, bf16[128,128]{0,1:T(8,128)(2,1)S(1)}, u32[]{:S(2)}, u32[]{:S(2)}) collective-permute-start(bf16[128,128]{0,1:T(8,128)(2,1)S(1)} %copy.30), channel_id=1, source_target_pairs={{0,1},{1,2},{2,3},{3,0},{4,5},{5,6},{6,7},{7,4},{8,9},{9,10},{10,1... | collective-permute-start | bytes 98312 | tf_op jit(solution)/shard_map/ppermute | solution.py:262
  178.4 57.0 %all-to-all-start.1 = ((bf16[64,128,128]{2,1,0:T(8,128)(2,1)}), bf16[64,128,128]{2,1,0:T(8,128)(2,1)S(1)}, u32[]{:S(2)}, u32[]{:S(2)}) async-start(bf16[64,128,128]{2,1,0:T(8,128)(2,1)} %products.3), calls=%async_computation.1 | async-start | bytes 4194304 | tf_op jit(solution)/shard_map/all_to_all | solution.py:228
  190.4 28.1 %copy-start.1 = (bf16[32,96,128]{2,1,0:T(8,128)(2,1)}, bf16[32,96,128]{2,1,0:T(8,128)(2,1)S(1)}, u32[]{:S(2)}) copy-start(bf16[32,96,128]{2,1,0:T(8,128)(2,1)S(1)} %get-tuple-element.19.refs_4_) | copy-start | bytes 2359300
  190.4 20.0 %collective-permute-start.3 = (bf16[32,96,128]{2,1,0:T(8,128)(2,1)S(1)}, bf16[32,96,128]{2,1,0:T(8,128)(2,1)}, u32[]{:S(2)}, u32[]{:S(2)}) collective-permute-start(bf16[32,96,128]{2,1,0:T(8,128)(2,1)S(1)} %get-tuple-element.18.refs_0_), channel_id=1, source_target_pairs={{0,1},{1,2},{2,3},{3,0},{4,5},{5,6},{6,7},{7,4},{8,9},{9,10},{10,1... | collective-permute-start | bytes 2359304 | tf_op jit(solution)/shard_map/ppermute | solution.py:233
  191.7 18.7 %collective-permute-start.6 = (bf16[32,96,128]{2,1,0:T(8,128)(2,1)S(1)}, bf16[32,96,128]{2,1,0:T(8,128)(2,1)}, u32[]{:S(2)}, u32[]{:S(2)}) collective-permute-start(bf16[32,96,128]{2,1,0:T(8,128)(2,1)S(1)} %get-tuple-element.19.refs_4_), channel_id=1, source_target_pairs={{0,3},{1,0},{2,1},{3,2},{4,7},{5,4},{6,5},{7,6},{8,11},{9,8},{10,9... | collective-permute-start | bytes 2359304 | tf_op jit(solution)/shard_map/ppermute | solution.py:234
  193.2 34.0 %collective-permute-start.4 = (bf16[32,96,128]{2,1,0:T(8,128)(2,1)S(1)}, bf16[32,96,128]{2,1,0:T(8,128)(2,1)S(1)}, u32[]{:S(2)}, u32[]{:S(2)}) collective-permute-start(bf16[32,96,128]{2,1,0:T(8,128)(2,1)S(1)} %get-tuple-element.19.refs_4_), channel_id=1, source_target_pairs={{0,1},{1,2},{2,3},{3,0},{4,5},{5,6},{6,7},{7,4},{8,9},{9,10},{10,1... | collective-permute-start | bytes 2359304 | tf_op jit(solution)/shard_map/ppermute | solution.py:235
  193.2 35.0 %collective-permute-start.5 = (bf16[32,96,128]{2,1,0:T(8,128)(2,1)S(1)}, bf16[32,96,128]{2,1,0:T(8,128)(2,1)S(1)}, u32[]{:S(2)}, u32[]{:S(2)}) collective-permute-start(bf16[32,96,128]{2,1,0:T(8,128)(2,1)S(1)} %get-tuple-element.18.refs_0_), channel_id=1, source_target_pairs={{0,3},{1,0},{2,1},{3,2},{4,7},{5,4},{6,5},{7,6},{8,11},{9,8},{10,9... | collective-permute-start | bytes 2359304 | tf_op jit(solution)/shard_map/ppermute | solution.py:236
  210.5 33.7 %collective-permute-start.11 = (bf16[32,96,128]{2,1,0:T(8,128)(2,1)}, bf16[32,96,128]{2,1,0:T(8,128)(2,1)}, u32[]{:S(2)}, u32[]{:S(2)}) collective-permute-start(bf16[32,96,128]{2,1,0:T(8,128)(2,1)} %collective-permute-done.3.refs_1_), channel_id=1, source_target_pairs={{0,1},{1,2},{2,3},{3,0},{4,5},{5,6},{6,7},{7,4},{8,9},{9,10},{10,1... | collective-permute-start | bytes 2359304 | tf_op jit(solution)/shard_map/ppermute | solution.py:243
  210.5 33.7 %collective-permute-start.12 = (bf16[32,96,128]{2,1,0:T(8,128)(2,1)}, bf16[32,96,128]{2,1,0:T(8,128)(2,1)}, u32[]{:S(2)}, u32[]{:S(2)}) collective-permute-start(bf16[32,96,128]{2,1,0:T(8,128)(2,1)} %collective-permute-done.6.refs_7_), channel_id=1, source_target_pairs={{0,3},{1,0},{2,1},{3,2},{4,7},{5,4},{6,5},{7,6},{8,11},{9,8},{10,9... | collective-permute-start | bytes 2359304 | tf_op jit(solution)/shard_map/ppermute | solution.py:244
  239.9 2.5 copy-start.8
  239.9 36.1 %copy-start = (bf16[8192,128]{1,0:T(8,128)(2,1)S(1)}, bf16[8192,128]{1,0:T(8,128)(2,1)}, u32[]{:S(2)}) copy-start(bf16[8192,128]{1,0:T(8,128)(2,1)} %param.10) | copy-start | bytes 6291460
  244.2 21.8 %all-to-all-start.2 = ((bf16[64,8,128]{2,1,0:T(8,128)(2,1)}), bf16[64,8,128]{2,1,0:T(8,128)(2,1)}, u32[]{:S(2)}, u32[]{:S(2)}) async-start(bf16[64,8,128]{2,1,0:T(8,128)(2,1)} %bitcast.31), calls=%async_computation.2 | async-start | bytes 262144 | tf_op jit(solution)/shard_map/all_to_all | solution.py:228
  255.7 17.5 %collective-permute-start.7 = (bf16[32,32,128]{2,1,0:T(8,128)(2,1)S(1)}, bf16[32,32,128]{2,1,0:T(8,128)(2,1)}, u32[]{:S(2)}, u32[]{:S(2)}) collective-permute-start(bf16[32,32,128]{2,1,0:T(8,128)(2,1)S(1)} %get-tuple-element.21.refs_0_), channel_id=1, source_target_pairs={{0,1},{1,2},{2,3},{3,0},{4,5},{5,6},{6,7},{7,4},{8,9},{9,10},{10,1... | collective-permute-start | bytes 786440 | tf_op jit(solution)/shard_map/ppermute | solution.py:233
  257.0 16.3 %collective-permute-start.8 = (bf16[32,32,128]{2,1,0:T(8,128)(2,1)S(1)}, bf16[32,32,128]{2,1,0:T(8,128)(2,1)}, u32[]{:S(2)}, u32[]{:S(2)}) collective-permute-start(bf16[32,32,128]{2,1,0:T(8,128)(2,1)S(1)} %get-tuple-element.22.refs_4_), channel_id=1, source_target_pairs={{0,1},{1,2},{2,3},{3,0},{4,5},{5,6},{6,7},{7,4},{8,9},{9,10},{10,1... | collective-permute-start | bytes 786440 | tf_op jit(solution)/shard_map/ppermute | solution.py:235
  257.9 15.3 %collective-permute-start.9 = (bf16[32,32,128]{2,1,0:T(8,128)(2,1)S(1)}, bf16[32,32,128]{2,1,0:T(8,128)(2,1)}, u32[]{:S(2)}, u32[]{:S(2)}) collective-permute-start(bf16[32,32,128]{2,1,0:T(8,128)(2,1)S(1)} %get-tuple-element.21.refs_0_), channel_id=1, source_target_pairs={{0,3},{1,0},{2,1},{3,2},{4,7},{5,4},{6,5},{7,6},{8,11},{9,8},{10,9... | collective-permute-start | bytes 786440 | tf_op jit(solution)/shard_map/ppermute | solution.py:236
  259.6 13.6 %collective-permute-start.10 = (bf16[32,32,128]{2,1,0:T(8,128)(2,1)S(1)}, bf16[32,32,128]{2,1,0:T(8,128)(2,1)}, u32[]{:S(2)}, u32[]{:S(2)}) collective-permute-start(bf16[32,32,128]{2,1,0:T(8,128)(2,1)S(1)} %get-tuple-element.22.refs_4_), channel_id=1, source_target_pairs={{0,3},{1,0},{2,1},{3,2},{4,7},{5,4},{6,5},{7,6},{8,11},{9,8},{10,9... | collective-permute-start | bytes 786440 | tf_op jit(solution)/shard_map/ppermute | solution.py:234
  267.6 17.0 %all-to-all-start.3 = ((bf16[64,8,128]{2,1,0:T(8,128)(2,1)}), bf16[64,8,128]{2,1,0:T(8,128)(2,1)}, u32[]{:S(2)}, u32[]{:S(2)}) async-start(bf16[64,8,128]{2,1,0:T(8,128)(2,1)} %broadcast_in_dim.12), calls=%async_computation.3 | async-start | bytes 262144 | tf_op jit(solution)/shard_map/all_to_all | solution.py:228
  273.2 13.0 %collective-permute-start.13 = (bf16[32,32,128]{2,1,0:T(8,128)(2,1)}, bf16[32,32,128]{2,1,0:T(8,128)(2,1)}, u32[]{:S(2)}, u32[]{:S(2)}) collective-permute-start(bf16[32,32,128]{2,1,0:T(8,128)(2,1)} %collective-permute-done.7.refs_1_), channel_id=1, source_target_pairs={{0,1},{1,2},{2,3},{3,0},{4,5},{5,6},{6,7},{7,4},{8,9},{9,10},{10,1... | collective-permute-start | bytes 786440 | tf_op jit(solution)/shard_map/ppermute | solution.py:243
  274.5 11.7 %collective-permute-start.14 = (bf16[32,32,128]{2,1,0:T(8,128)(2,1)}, bf16[32,32,128]{2,1,0:T(8,128)(2,1)}, u32[]{:S(2)}, u32[]{:S(2)}) collective-permute-start(bf16[32,32,128]{2,1,0:T(8,128)(2,1)} %collective-permute-done.10.refs_7_), channel_id=1, source_target_pairs={{0,3},{1,0},{2,1},{3,2},{4,7},{5,4},{6,5},{7,6},{8,11},{9,8},{10,9... | collective-permute-start | bytes 786440 | tf_op jit(solution)/shard_map/ppermute | solution.py:244
  276.0 1.1 copy-start.2
  (6 other events, 5.8 us)
Sparse Core Ops, SparseCore 0:
  37.4 86.6 all-gather.2
